TPU v7x, 32 devices: a whole 2x2x4 slice. The times are simulated.
32 devices in a mesh: row: 8 (over z, x), mp: 4 (over y, core).
Axes of the slice: x: 2, y: 2, z: 4, core: 2. Of those that a mesh axis runs over, the one named last changes fastest.
Arguments:
- token_ids: int32 [64, 128], P('row'), may hold values from 0 to 511
- set_lengths: int32 [64], P('row'), may hold values from 32 to 128
- live_counts: int32 [8], replicated, may hold values from 1 to 8, 32 in all
- embed_table: bfloat16 [512, 5120], replicated, may hold values from -3 to 3
- position_table: bfloat16 [128, 5120], replicated, may hold values from -3 to 3
- norm_gain: float32 [5120], replicated, may hold values from 0.1 to 1.9
- w_query: bfloat16 [5120, 5120], P('row', 'mp')
- w_key: bfloat16 [5120, 5120], P('row', 'mp')
- w_value: bfloat16 [5120, 5120], P('row', 'mp'), may hold values from -0.078125 to 0.078125
- w_out: bfloat16 [5120, 5120], P('mp', 'row'), may hold values from -0.078125 to 0.078125
Outputs:
- verified: bfloat16 [64, 128, 5120], P('row', None, 'mp')
Inputs may be any that keep to these rules, and one draw needn't show every extreme that they name: Owner group g has live_counts[g] live sets, its first slots; the counts sum to 32 and one group holds 8. `set_lengths`: positions at or past a set's length are padding.
All inputs are finite; a program needn't handle non-finite values.
Results may differ from a plain program's by a relative error of at most 0.017.
Values may be sent and summed in bfloat16 or wider, within the bound.
A program may use at most 128 MiB of HBM per device.

v0:
```python
import jax
import jax.numpy as jnp
from jax import lax
from jax.sharding import PartitionSpec as P

DH = 128


def prepare(group_ids, embed_table, position_table, norm_gain):
    summed = (
        jnp.take(embed_table, group_ids, axis=0).astype(jnp.float32)
        + position_table.astype(jnp.float32)[None]
    )
    stored = lax.optimization_barrier(summed.astype(jnp.bfloat16))
    widened = stored.astype(jnp.float32)
    inverse = lax.rsqrt(jnp.mean(widened * widened, axis=-1, keepdims=True) + 1e-05)
    normed = (widened * inverse * norm_gain).astype(jnp.bfloat16)
    return (stored, normed)


def attend(query, keys, values, group_lengths):
    set_count = group_lengths.shape[0]
    seq_len = query.shape[0] // set_count
    q_four = query.reshape(set_count, seq_len, -1, DH)
    k_four = keys.reshape(set_count, seq_len, -1, DH)
    v_four = values.reshape(set_count, seq_len, -1, DH)
    scores = jnp.einsum(
        "sqhd,skhd->shqk", q_four, k_four, preferred_element_type=jnp.float32
    ) * DH ** (-0.5)
    valid = jnp.arange(seq_len)[None, :] < group_lengths[:, None]
    scores = jnp.where(valid[:, None, None, :], scores, -1e30)
    highest = jnp.max(scores, axis=-1, keepdims=True)
    expo = jnp.exp(scores - highest)
    weights = (expo / jnp.sum(expo, axis=-1, keepdims=True)).astype(jnp.bfloat16)
    mixed = jnp.einsum("shqk,skhd->sqhd", weights, v_four, preferred_element_type=jnp.float32)
    return mixed.astype(jnp.bfloat16).reshape(set_count * seq_len, -1)


def verify(
    group_ids,
    group_lengths,
    live,
    embed_table,
    position_table,
    norm_gain,
    w_query,
    w_key,
    w_value,
    w_out,
):
    set_count, seq_len = group_ids.shape
    stored, normed = prepare(group_ids, embed_table, position_table, norm_gain)
    flat = normed.reshape(set_count * seq_len, -1)
    query = jnp.dot(
        flat, lax.all_gather(w_query, "row", axis=0, tiled=True), preferred_element_type=jnp.float32
    )
    keys = jnp.dot(
        flat, lax.all_gather(w_key, "row", axis=0, tiled=True), preferred_element_type=jnp.float32
    )
    values = jnp.dot(
        flat, lax.all_gather(w_value, "row", axis=0, tiled=True), preferred_element_type=jnp.float32
    )
    mixed = attend(
        query.astype(jnp.bfloat16),
        keys.astype(jnp.bfloat16),
        values.astype(jnp.bfloat16),
        group_lengths,
    )
    partial_value = jnp.dot(
        mixed, lax.all_gather(w_out, "row", axis=1, tiled=True), preferred_element_type=jnp.float32
    )
    summed = lax.psum_scatter(
        partial_value.astype(jnp.bfloat16), "mp", scatter_dimension=1, tiled=True
    ).astype(jnp.float32)
    features = summed.shape[1]
    residual = lax.dynamic_slice_in_dim(
        stored.reshape(set_count * seq_len, -1), lax.axis_index("mp") * features, features, 1
    )
    valid = jnp.arange(seq_len)[None, :] < group_lengths[:, None]
    keep = (live[:, None] & valid).reshape(-1, 1).astype(jnp.float32)
    output = ((residual.astype(jnp.float32) + summed) * keep).astype(jnp.bfloat16)
    return output.reshape(set_count, seq_len, features)


def on_device(
    token_ids,
    set_lengths,
    live_counts,
    embed_table,
    position_table,
    norm_gain,
    w_query,
    w_key,
    w_value,
    w_out,
):
    slot_count, seq_len = token_ids.shape
    my_group = lax.axis_index("row")
    own_live = jnp.arange(slot_count) < live_counts[my_group]
    return verify(
        token_ids,
        set_lengths,
        own_live,
        embed_table,
        position_table,
        norm_gain,
        w_query,
        w_key,
        w_value,
        w_out,
    )


def solution(mesh):
    in_specs = (
        P("row", None),
        P("row"),
        P(),
        P(),
        P(),
        P(),
        P("row", "mp"),
        P("row", "mp"),
        P("row", "mp"),
        P("mp", "row"),
    )
    out_specs = P("row", None, "mp")
    return jax.shard_map(
        on_device, mesh=mesh, in_specs=in_specs, out_specs=out_specs, check_vma=False
    )
```

profile of v0, /device:TPU:0, one launch (start us, length us, event | category | flops | bytes accessed | tf_op | source)
XLA Modules:
  0.0 860.7 jit_solution(6086895719423092631)
XLA Ops:
  6.5 0.0 copy-start.3
  6.5 0.0 all-gather.7.cloned.1.call-start
  6.5 0.7 all-gather.7.cloned.1.call-update
  7.3 0.0 all-gather.9.cloned.1.call-start
  7.3 0.7 all-gather.9.cloned.1.call-update
  8.0 0.0 all-gather.5.cloned.1.call-start
  8.1 0.7 all-gather.5.cloned.1.call-update
  8.7 0.0 all-gather.11.cloned.1.call-start
  8.8 0.5 all-gather.11.cloned.1.call-update
  9.3 0.0 reduce-scatter.2.cloned.1.call-start
  9.4 1.6 convert_element_type.57
  10.9 0.0 copy-done.3
  11.0 21.7 %gather_fusion = bf16[1024,5120]{1,0:T(8,128)(2,1)} fusion(bf16[512,5120]{1,0:T(8,128)(2,1)} %param.13, s32[1024]{0:T(1024)S(1)} %bitcast_clamp_fusion), kind=kCustom, calls=%fused_computation | custom fusion | bytes 20975616 | tf_op jit(solution)/shard_map/jit(_take)/gather | solution.py:11
  32.7 0.0 copy-start.5
  32.7 0.0 copy-start.4
  32.7 0.0 copy-start.2
  32.8 11.1 %add_convert_fusion = bf16[8,128,5120]{2,1,0:T(8,128)(2,1)} fusion(f32[128,5120]{1,0:T(8,128)S(1)} %convert_element_type.57, bf16[8,128,5120]{2,1,0:T(8,128)(2,1)} %bitcast.26, pred[8,128]{1,0:T(8,128)(4,1)S(1)} %compare_and_fusion), kind=kLoop, calls=%fused_computation.7 | loop fusion | flops 20971520 | bytes 23593984 | tf_op jit(solution)/shard_map/convert_element_type | solution.py:14
  43.8 0.0 copy-done.5
  43.8 0.6 dynamic_slice.7
  44.4 0.6 iota_compare_fusion.1
  45.1 0.0 copy-done.4
  45.1 0.1 convert_bitcast_fusion.1
  45.1 0.0 copy-start
  45.1 6.3 fusion.1
  51.4 0.0 copy-done.2
  51.4 0.8 copy-done
  52.2 5.8 fusion.3
  58.0 137.1 %all-gather.7.cloned.1.call-done = bf16[5120,1280]{1,0:T(8,128)(2,1)} async-done(((bf16[640,1280]{1,0:T(8,128)(2,1)}), bf16[5120,1280]{1,0:T(8,128)(2,1)}) %all-gather.7.cloned.1.call-update) | async-done | bytes 13107216 | tf_op jit(solution)/shard_map/all_gather | solution.py:55
  195.1 17.4 %convolution_convert_fusion.2 = bf16[1024,1280]{1,0:T(8,128)(2,1)S(1)} fusion(bf16[1024,5120]{1,0:T(8,128)(2,1)} %bitcast.27, bf16[5120,1280]{1,0:T(8,128)(2,1)} %all-gather.7.cloned.1.call-done), kind=kOutput, calls=%fused_computation.15 | convolution fusion | flops 13423083520 | bytes 26214400 | tf_op jit(solution)/shard_map/dot_general | solution.py:54
  212.5 3.2 reshape.103
  215.7 162.7 %all-gather.9.cloned.1.call-done = bf16[5120,1280]{1,0:T(8,128)(2,1)} async-done(((bf16[640,1280]{1,0:T(8,128)(2,1)}), bf16[5120,1280]{1,0:T(8,128)(2,1)}) %all-gather.9.cloned.1.call-update) | async-done | bytes 13107216 | tf_op jit(solution)/shard_map/all_gather | solution.py:58
  378.3 17.3 %convolution_convert_fusion.1 = bf16[1024,1280]{1,0:T(8,128)(2,1)S(1)} fusion(bf16[1024,5120]{1,0:T(8,128)(2,1)} %bitcast.28, bf16[5120,1280]{1,0:T(8,128)(2,1)} %all-gather.9.cloned.1.call-done), kind=kOutput, calls=%fused_computation.14 | convolution fusion | flops 13423083520 | bytes 26214400 | tf_op jit(solution)/shard_map/dot_general | solution.py:57
  395.7 3.4 reshape.104
  399.1 162.5 %all-gather.5.cloned.1.call-done = bf16[5120,1280]{1,0:T(8,128)(2,1)} async-done(((bf16[640,1280]{1,0:T(8,128)(2,1)}), bf16[5120,1280]{1,0:T(8,128)(2,1)}) %all-gather.5.cloned.1.call-update) | async-done | bytes 13107216 | tf_op jit(solution)/shard_map/all_gather | solution.py:61
  561.6 17.4 %convolution_convert_fusion.3 = bf16[1024,1280]{1,0:T(8,128)(2,1)S(1)} fusion(bf16[1024,5120]{1,0:T(8,128)(2,1)} %bitcast.29, bf16[5120,1280]{1,0:T(8,128)(2,1)} %all-gather.5.cloned.1.call-done), kind=kOutput, calls=%fused_computation.16 | convolution fusion | flops 13423083520 | bytes 26214400 | tf_op jit(solution)/shard_map/dot_general | solution.py:60
  579.0 3.2 reshape.102
  582.2 5.5 fusion.8
  587.6 0.0 copy-start.1
  587.6 2.4 fusion.20
  590.1 0.0 copy-done.1
  590.1 1.3 convert_bitcast_fusion
  591.3 1.9 copy.22
  593.3 151.5 %all-gather.11.cloned.1.call-done = bf16[1280,5120]{1,0:T(8,128)(2,1)} async-done(((bf16[1280,640]{1,0:T(8,128)(2,1)}), bf16[1280,5120]{1,0:T(8,128)(2,1)}) %all-gather.11.cloned.1.call-update) | async-done | bytes 13107216 | tf_op jit(solution)/shard_map/all_gather | solution.py:70
  744.7 20.9 %convolution_convert_fusion = bf16[1024,5120]{1,0:T(8,128)(2,1)} fusion(bf16[1280,5120]{1,0:T(8,128)(2,1)} %all-gather.11.cloned.1.call-done, bf16[160,8,8,128]{3,2,1,0:T(8,128)(2,1)S(1)} %bitcast.30), kind=kOutput, calls=%fused_computation.8 | convolution fusion | flops 13427015680 | bytes 26214400 | tf_op jit(solution)/shard_map/dot_general | solution.py:69
  765.7 0.0 reduce-scatter.2.cloned.1.call-update
  765.7 83.6 %reduce-scatter.2.cloned.1.call-done = bf16[1024,1280]{1,0:T(8,128)(2,1)} async-done(((bf16[1024,5120]{1,0:T(8,128)(2,1)}), bf16[1024,1280]{1,0:T(8,128)(2,1)}) %reduce-scatter.2.cloned.1.call-update) | async-done | bytes 2621456 | tf_op jit(solution)/shard_map/reduce_scatter | solution.py:72
  849.3 4.8 multiply_convert_fusion
  (3 shorter events, 0.0 us)
Async XLA Ops:
  6.5 4.4 copy-start.3
  6.5 188.6 %all-gather.7.cloned.1.call-start = ((), (), s32[]{:S(2)}) async-start(), calls=%async_computation.2 | async-start | bytes 14745600 | tf_op jit(solution)/shard_map/all_gather | solution.py:55
  7.3 371.1 %all-gather.9.cloned.1.call-start = ((), (), s32[]{:S(2)}) async-start(), calls=%async_computation.3 | async-start | bytes 14745600 | tf_op jit(solution)/shard_map/all_gather | solution.py:58
  8.0 553.6 %all-gather.5.cloned.1.call-start = ((), (), s32[]{:S(2)}) async-start(), calls=%async_computation.1 | async-start | bytes 14745600 | tf_op jit(solution)/shard_map/all_gather | solution.py:61
  8.7 736.0 %all-gather.11.cloned.1.call-start = ((), (), s32[]{:S(2)}) async-start(), calls=%async_computation.4 | async-start | bytes 14745600 | tf_op jit(solution)/shard_map/all_gather | solution.py:70
  9.3 840.0 %reduce-scatter.2.cloned.1.call-start = ((), (), s32[]{:S(2)}) async-start(), calls=%async_computation.5 | async-start | bytes 13107200 | tf_op jit(solution)/shard_map/reduce_scatter | solution.py:72
  32.7 11.1 %copy-start.5 = (s32[8]{0:T(128)S(1)}, s32[8]{0:T(128)}, u32[]{:S(2)}) copy-start(s32[8]{0:T(128)} %param.12) | copy-start | bytes 100
  32.7 12.3 %copy-start.4 = (s32[8]{0:T(128)S(1)}, s32[8]{0:T(128)}, u32[]{:S(2)}) copy-start(s32[8]{0:T(128)} %param.11) | copy-start | bytes 100
  32.7 18.7 %copy-start.2 = (f32[5120]{0:T(1024)S(1)}, f32[5120]{0:T(1024)}, u32[]{:S(2)}) copy-start(f32[5120]{0:T(1024)} %param.15) | copy-start | bytes 61444
  45.1 7.1 copy-start
  587.6 2.4 copy-start.1
Sparse Core Ops, SparseCore 0:
  9.5 185.5 all-gather.6
  197.3 180.9 all-gather.8
  380.5 180.9 all-gather.4
  563.7 181.0 all-gather.10
  765.8 83.4 reduce-scatter.1
where the time goes:
time: 861 us
  waiting for transfers between devices  700 us (81%)
  matrix products  79.8 us (9%)
  local copies, waits for them, and re-layouts  34.8 us (4%)
  other arithmetic  32.7 us (4%)
  between operations  13.3 us (2%)
    all_gather x1, waiting for transfers between devices, verify(): lax.all_gather(w_key, 'row', axis=0, tiled=True)  163 us
    all_gather x1, waiting for transfers between devices, verify(): lax.all_gather(w_value, 'row', axis=0, tiled=True)  162 us
    all_gather x1, waiting for transfers between devices, verify(): lax.all_gather(w_out, 'row', axis=1, tiled=True)  151 us
    all_gather x1, waiting for transfers between devices, verify(): lax.all_gather(w_query, 'row', axis=0, tiled=True)  137 us
    reduce_scatter x1, waiting for transfers between devices, verify(): lax.psum_scatter(partial_value.astype(jnp.bfloat16), 'mp', scatter_dimens...  83.6 us
    gather x1, local copies, waits for them, and re-layouts, prepare(): jnp.take(embed_table, group_ids, axis=0).astype(jnp.float32)  21.7 us
    dot_general x1, matrix products, verify(): jnp.dot(mixed, lax.all_gather(w_out, 'row', axis=1, tiled=True), preferre...  20.9 us
    dot_general x1, matrix products, verify(): jnp.dot(flat, lax.all_gather(w_value, 'row', axis=0, tiled=True), preferr...  17.4 us
  transfers between devices with their start and end apart: 5, of which 5 were waited for; matrix products, arithmetic and copies ran while one was open for 14% of the time, Pallas kernels for 0%

commit v1 on v0

v1 whole, which is shorter than its diff:
```python
import functools
import jax
import jax.numpy as jnp
from jax import lax
from jax.experimental import pallas as pl
from jax.experimental.pallas import tpu as pltpu
from jax.sharding import PartitionSpec as P

DH = 128


def attend_kernel(heads, vocab, lengths_ref, live_ref, ids_ref, inv_ref, table_ref, out_ref):
    s = pl.program_id(0)
    seq = out_ref.shape[0]
    width = heads * DH
    length = lengths_ref[s]

    @pl.when(live_ref[s] == 0)
    def _():
        out_ref[...] = jnp.zeros_like(out_ref)

    @pl.when(live_ref[s] != 0)
    def _():
        ids = ids_ref[...].reshape(seq, 1)
        cols = lax.broadcasted_iota(jnp.int32, (seq, vocab + seq), 1)
        rows = lax.broadcasted_iota(jnp.int32, (seq, vocab + seq), 0)
        pick = jnp.where((cols == ids) | (cols == rows + vocab), 1.0, 0.0).astype(jnp.bfloat16)
        inv = inv_ref[...].reshape(seq, 1)
        masked = lax.broadcasted_iota(jnp.int32, (seq, seq), 1) >= length


        pieces = {}
        for part in range(3):
            at = 0
            while at < width:
                step = min(2 * DH, width - at)
                got = jnp.dot(
                    pick, table_ref[:, part * width + at:part * width + at + step],
                    preferred_element_type=jnp.float32,
                )
                got = (got * inv).astype(jnp.bfloat16)
                for k in range(step // DH):
                    pieces[part, at // DH + k] = got[:, k * DH:(k + 1) * DH]
                at += step
        for h in range(heads):
            q, k, v = pieces[0, h], pieces[1, h], pieces[2, h]
            scores = lax.dot_general(
                q, k, (((1,), (1,)), ((), ())), preferred_element_type=jnp.float32
            ) * DH ** (-0.5)
            scores = jnp.where(masked, -1e30, scores)
            expo = jnp.exp(scores - jnp.max(scores, axis=-1, keepdims=True))
            weights = (expo / jnp.sum(expo, axis=-1, keepdims=True)).astype(jnp.bfloat16)
            mixed = jnp.dot(weights, v, preferred_element_type=jnp.float32)
            out_ref[:, h * DH:(h + 1) * DH] = mixed.astype(jnp.bfloat16)


def attend(ids, lengths, live, inv, table, heads, vocab):
    sets, seq = ids.shape
    width = heads * DH
    grid_spec = pltpu.PrefetchScalarGridSpec(
        num_scalar_prefetch=2,
        grid=(sets,),
        in_specs=[
            pl.BlockSpec((None, seq, 1), lambda s, *_: (s, 0, 0)),
            pl.BlockSpec((None, seq, 1), lambda s, *_: (s, 0, 0)),
            pl.BlockSpec((vocab + seq, 3 * width), lambda s, *_: (0, 0)),
        ],
        out_specs=pl.BlockSpec((seq, width), lambda s, *_: (s, 0)),
    )
    return pl.pallas_call(
        functools.partial(attend_kernel, heads, vocab),
        out_shape=jax.ShapeDtypeStruct((sets * seq, width), jnp.bfloat16),
        grid_spec=grid_spec,
        compiler_params=pltpu.CompilerParams(vmem_limit_bytes=40 * 1024 * 1024),
        cost_estimate=pl.CostEstimate(
            flops=2 * sets * seq * (vocab + seq) * 3 * width,
            bytes_accessed=2 * (vocab + seq) * 3 * width,
            transcendentals=sets * seq * seq * heads,
        ),
    )(lengths, live, ids[..., None], inv[..., None], table)


def on_device(
    token_ids, set_lengths, live_counts, embed_table, position_table, norm_gain,
    w_query, w_key, w_value, w_out,
):
    sets, seq = token_ids.shape
    vocab, d = embed_table.shape
    me, part = lax.axis_index("row"), lax.axis_index("mp")
    depth, width = w_query.shape
    heads = width // DH

    rows = jnp.concatenate([
        lax.dynamic_slice_in_dim(embed_table, me * depth, depth, 1),
        lax.dynamic_slice_in_dim(position_table, me * depth, depth, 1),
    ], axis=0).astype(jnp.float32)
    rows = (rows * lax.dynamic_slice_in_dim(norm_gain, me * depth, depth)).astype(jnp.bfloat16)
    partial = jnp.concatenate([
        jnp.dot(rows, w, preferred_element_type=jnp.float32).astype(jnp.bfloat16)
        for w in (w_query, w_key, w_value)
    ], axis=1)
    table = lax.psum(partial, "row")

    out_full = lax.all_gather(w_out, "row", axis=1, tiled=True)

    pick = (token_ids.reshape(-1, 1) == jnp.arange(vocab)[None]).astype(jnp.bfloat16)
    picked = jnp.dot(pick, embed_table, preferred_element_type=jnp.float32)
    stored = (
        picked.reshape(sets, seq, d) + position_table.astype(jnp.float32)[None]
    ).astype(jnp.bfloat16)
    widened = stored.astype(jnp.float32)
    inv = lax.rsqrt(jnp.mean(widened * widened, axis=-1) + 1e-05)

    live = jnp.arange(sets) < live_counts[me]
    mixed = attend(
        token_ids, set_lengths, live.astype(jnp.int32), inv, table, heads, vocab
    )
    partial_out = jnp.dot(mixed, out_full, preferred_element_type=jnp.float32).astype(jnp.bfloat16)
    summed = lax.psum_scatter(
        partial_out, "mp", scatter_dimension=1, tiled=True
    ).astype(jnp.float32)
    features = summed.shape[1]
    residual = lax.dynamic_slice_in_dim(
        stored.reshape(sets * seq, d), part * features, features, 1
    ).astype(jnp.float32)
    valid = jnp.arange(seq)[None, :] < set_lengths[:, None]
    keep = (live[:, None] & valid).reshape(-1, 1)
    output = jnp.where(keep, residual + summed, 0.0).astype(jnp.bfloat16)
    return output.reshape(sets, seq, features)


def solution(mesh):
    in_specs = (
        P("row", None), P("row"), P(), P(), P(), P(),
        P("row", "mp"), P("row", "mp"), P("row", "mp"), P("mp", "row"),
    )
    return jax.shard_map(
        on_device, mesh=mesh, in_specs=in_specs, out_specs=P("row", None, "mp"), check_vma=False
    )
```

time: 861 us -> 494 us (0.57)
  waiting for transfers between devices: 700 us -> 401 us
  matrix products: 79.8 us -> 36.3 us
  local copies, waits for them, and re-layouts: 34.8 us -> 8.24 us
  Pallas kernels: 0 us -> 23.9 us
  other arithmetic: 32.7 us -> 10.3 us
    all_gather x4 -> x1, waiting for transfers between devices: 614 us -> 157 us  [on_device(): out_full = lax.all_gather(w_out, 'row', axis=1, tiled=True)]
    psum x0 -> x1, waiting for transfers between devices: none -> 161 us  [on_device(): table = lax.psum(partial, 'row')]
    dot_general x6 -> x5, matrix products: 79.8 us -> 36.3 us  [the longest x1 19.9 us: on_device(): jnp.dot(mixed, out_full, preferred_element_type=jnp.float32)]
    pallas_call x0 -> x1, Pallas kernels: none -> 23.9 us  [attend(): pl.pallas_call(functools.partial(attend_kernel, heads, vocab), out_shape=...]
    gather x1 -> x0, local copies, waits for them, and re-layouts: 21.7 us -> none  [prepare(): jnp.take(embed_table, group_ids, axis=0).astype(jnp.float32)]
    convert_element_type x5 -> x3, other arithmetic: 23.3 us -> 7.26 us  [the longest x1 4.94 us: on_device(): output = jnp.where(keep, residual + summed, 0.0).astype(jnp.bfloat16)]
    reshape x3 -> x0, local copies, waits for them, and re-layouts: 9.75 us -> none  [the longest x1 3.39 us: attend(): k_four = keys.reshape(set_count, seq_len, -1, DH)]
  transfers between devices with their start and end apart: 5 -> 3, of which waited for: 5 -> 3; matrix products, arithmetic and copies ran while one was open for 14% -> 3% of each run, Pallas kernels for 0% -> 5%
where the time goes in v1:
time: 494 us; the launch traced here: 493 us
  waiting for transfers between devices  401 us (81%)
  matrix products  36.3 us (7%)
  Pallas kernels  23.9 us (5%)
  between operations  13.2 us (3%)
  other arithmetic  10.3 us (2%)
  local copies, waits for them, and re-layouts  8.24 us (2%)
    psum x1, waiting for transfers between devices, on_device(): table = lax.psum(partial, 'row')  161 us
    all_gather x1, waiting for transfers between devices, on_device(): out_full = lax.all_gather(w_out, 'row', axis=1, tiled=True)  157 us
    reduce_scatter x1, waiting for transfers between devices, on_device(): lax.psum_scatter(partial_out, 'mp', scatter_dimension=1, tiled=True)  83 us
    pallas_call x1, Pallas kernels, attend(): pl.pallas_call(functools.partial(attend_kernel, heads, vocab), out_shape=...  23.9 us
    dot_general x1, matrix products, on_device(): jnp.dot(mixed, out_full, preferred_element_type=jnp.float32)  19.9 us
    dot_general x1, matrix products, on_device(): picked = jnp.dot(pick, embed_table, preferred_element_type=jnp.float32)  12.1 us
  transfers between devices with their start and end apart: 3, of which 3 were waited for; matrix products, arithmetic and copies ran while one was open for 3% of the time, Pallas kernels for 5%

profile of v1, /device:TPU:0, one launch (start us, length us, event | category | flops | bytes accessed | tf_op | source)
XLA Modules:
  0.0 493.4 jit_solution(12891614387099044316)
XLA Ops:
  6.5 0.0 copy-start
  6.5 0.0 all-reduce.2.cloned.1.call-start
  6.5 1.3 constant_dynamic-slice_fusion.1
  7.8 0.9 constant_dynamic-slice_fusion
  8.8 0.8 dynamic_slice.19
  9.5 0.0 copy-done
  9.5 0.0 copy-start.7
  9.5 1.4 convolution_convert_fusion.1
  11.0 0.0 copy-done.7
  11.0 0.0 copy-start.8
  11.0 1.5 convolution_convert_fusion.2
  12.5 0.0 copy-done.8
  12.5 1.5 convolution_convert_fusion.3
  13.9 2.3 pad_maximum_fusion
  16.3 0.0 copy-start.5
  16.3 0.0 all-reduce.2.cloned.1.call-update
  16.3 0.0 copy-start.6
  16.3 0.0 all-gather.2.cloned.1.call-start
  16.4 0.7 all-gather.2.cloned.1.call-update
  17.1 0.2 reduce-scatter.2.cloned.1.call-start
  17.3 0.3 copy-done.5
  17.6 1.8 convert_element_type.43
  19.4 0.0 copy-done.6
  19.4 0.0 copy-start.9
  19.4 0.0 copy-start.2
  19.4 12.1 %multiply_reduce_fusion = (f32[1024]{0:T(1024)S(1)}, bf16[1024,5120]{1,0:T(8,128)(2,1)}) fusion(f32[128,5120]{1,0:T(8,128)} %convert_element_type.43, bf16[512,5120]{1,0:T(8,128)(2,1)} %param.13, s32[1024]{0:T(1024)S(1)} %bitcast.18), kind=kOutput, calls=%fused_computation.2 | convolution fusion | flops 5395446784 | bytes 18358272 | tf_op jit(solution)/shard_map/dot_general | solution.py:107
  31.5 0.2 copy.12.inv_ref
  31.7 0.2 copy.11.ids_ref
  31.9 0.0 copy-done.9
  32.0 0.6 dynamic_slice.15
  32.5 0.6 fusion.7.live_ref
  33.1 160.9 %all-reduce.2.cloned.1.call-done.table_ref = bf16[640,3840]{1,0:T(8,128)(2,1)} async-done(((bf16[640,3840]{1,0:T(8,128)(2,1)}), bf16[640,3840]{1,0:T(8,128)(2,1)}) %all-reduce.2.cloned.1.call-update) | async-done | bytes 4915216 | tf_op jit(solution)/shard_map/psum | solution.py:102
  194.0 0.0 copy-done.2
  194.0 0.0 copy-start.3
  194.0 2.4 copy-done.3
  196.4 23.9 %shard_map.100 = bf16[1024,1280]{1,0:T(8,128)(2,1)S(1)} custom-call(s32[8]{0:T(128)S(1)} %copy-done.2, s32[8]{0:T(128)S(1)} %fusion.7.live_ref, s32[8,128,1]{2,1,0:T(8,128)S(1)} %copy.11.ids_ref, f32[8,128,1]{2,1,0:T(8,128)S(1)} %copy.12.inv_ref, bf16[640,3840]{1,0:T(8,128)(2,1)S(1)} %copy-done.3), custom_call_target="tpu_custom_call" | custom-call | flops 5033164800 | bytes 4915200 | tf_op jit(solution)/shard_map/pallas_call | solution.py:70
  220.3 0.0 copy-start.4
  220.3 1.5 copy-done.4
  221.8 156.6 %all-gather.2.cloned.1.call-done = bf16[1280,5120]{1,0:T(8,128)(2,1)} async-done(((bf16[1280,640]{1,0:T(8,128)(2,1)}), bf16[1280,5120]{1,0:T(8,128)(2,1)}) %all-gather.2.cloned.1.call-update) | async-done | bytes 13107216 | tf_op jit(solution)/shard_map/all_gather | solution.py:104
  378.4 19.9 %convolution_convert_fusion = bf16[1024,5120]{1,0:T(8,128)(2,1)} fusion(bf16[1024,1280]{1,0:T(8,128)(2,1)} %copy-done.4, bf16[1280,5120]{1,0:T(8,128)(2,1)} %all-gather.2.cloned.1.call-done), kind=kOutput, calls=%fused_computation.3 | convolution fusion | flops 13427015680 | bytes 26214400 | tf_op jit(solution)/shard_map/dot_general | solution.py:118
  398.3 0.0 reduce-scatter.2.cloned.1.call-update
  398.3 0.6 iota_compare_fusion.3
  398.9 0.1 fusion.3
  398.9 83.0 %reduce-scatter.2.cloned.1.call-done = bf16[1024,1280]{1,0:T(8,128)(2,1)} async-done(((bf16[1024,5120]{1,0:T(8,128)(2,1)}), bf16[1024,1280]{1,0:T(8,128)(2,1)}) %reduce-scatter.2.cloned.1.call-update) | async-done | bytes 2621456 | tf_op jit(solution)/shard_map/reduce_scatter | solution.py:119
  481.9 0.0 copy-start.1
  481.9 4.9 %select_convert_fusion = bf16[1024,1280]{1,0:T(8,128)(2,1)} fusion(bf16[1024,1280]{1,0:T(8,128)(2,1)} %reduce-scatter.2.cloned.1.call-done, bf16[1024,5120]{1,0:T(8,128)(2,1)} %get-tuple-element.6, s32[]{:T(128)S(6)} %select_n.16, pred[1024]{0:T(1024)(128)(4,1)S(1)} %fusion.3), kind=kLoop, calls=%fused_computation.4 | loop fusion | flops 6553600 | bytes 7865348 | tf_op jit(solution)/shard_map/convert_element_type | solution.py:128
  486.9 0.0 copy-done.1
  (1 shorter events, 0.0 us)
Async XLA Ops:
  6.5 3.0 copy-start
  6.5 187.5 %all-reduce.2.cloned.1.call-start = ((), (), s32[]{:S(2)}) async-start(), calls=%async_computation.1 | async-start | bytes 9830400 | tf_op jit(solution)/shard_map/psum | solution.py:102
  9.5 1.5 copy-start.7
  11.0 1.5 copy-start.8
  16.3 1.3 copy-start.5
  16.3 3.0 copy-start.6
  16.3 362.1 %all-gather.2.cloned.1.call-start = ((), (), s32[]{:S(2)}) async-start(), calls=%async_computation.2 | async-start | bytes 14745600 | tf_op jit(solution)/shard_map/all_gather | solution.py:104
  17.1 464.9 %reduce-scatter.2.cloned.1.call-start = ((), (), s32[]{:S(2)}) async-start(), calls=%async_computation.3 | async-start | bytes 13107200 | tf_op jit(solution)/shard_map/reduce_scatter | solution.py:119
  19.4 12.6 %copy-start.9 = (s32[8]{0:T(128)S(1)}, s32[8]{0:T(128)}, u32[]{:S(2)}) copy-start(s32[8]{0:T(128)} %param.12) | copy-start | bytes 100
  19.4 174.6 %copy-start.2 = (s32[8]{0:T(128)S(1)}, s32[8]{0:T(128)}, u32[]{:S(2)}) copy-start(s32[8]{0:T(128)} %lengths_ref.1) | copy-start | bytes 100
  194.0 2.4 copy-start.3
  220.3 1.5 copy-start.4
  481.9 4.9 %copy-start.1 = (bf16[640,1280]{1,0:T(8,128)(2,1)S(1)}, bf16[640,1280]{1,0:T(8,128)(2,1)}, u32[]{:S(2)}) copy-start(bf16[640,1280]{1,0:T(8,128)(2,1)} %param.18) | copy-start | bytes 4915204
Sparse Core Ops, SparseCore 0:
  16.4 177.5 all-reduce.1
  196.5 181.8 all-gather.1
  398.4 83.4 reduce-scatter.1

commit v2 on v1

--- a/solution.py
+++ b/solution.py
@@ -35,7 +35,7 @@
             while at < width:
                 step = min(2 * DH, width - at)
                 got = jnp.dot(
-                    pick, table_ref[:, part * width + at:part * width + at + step],
+                    pick, table_ref[:vocab + seq, part * width + at:part * width + at + step],
                     preferred_element_type=jnp.float32,
                 )
                 got = (got * inv).astype(jnp.bfloat16)
@@ -63,7 +63,7 @@
         in_specs=[
             pl.BlockSpec((None, seq, 1), lambda s, *_: (s, 0, 0)),
             pl.BlockSpec((None, seq, 1), lambda s, *_: (s, 0, 0)),
-            pl.BlockSpec((vocab + seq, 3 * width), lambda s, *_: (0, 0)),
+            pl.BlockSpec(table.shape, lambda s, *_: (0, 0)),
         ],
         out_specs=pl.BlockSpec((seq, width), lambda s, *_: (s, 0)),
     )
@@ -80,8 +80,117 @@
     )(lengths, live, ids[..., None], inv[..., None], table)
 
 
+def flip(me, bit):
+    return me + (1 - 2 * (lax.rem(me // (1 << bit), 2))) * (1 << bit)
+
+
+def sum_kernel(levels, chunk, part_ref, out_ref, land, acc, send_sem, recv_sem):
+    me = lax.axis_index("row")
+    rows, cols = part_ref.shape
+    chunks = cols // chunk
+    count = len(levels)
+
+    barrier = pltpu.get_barrier_semaphore()
+    for bit in range(count):
+        pl.semaphore_signal(
+            barrier, inc=1, device_id={"row": flip(me, bit)}, device_id_type=pl.DeviceIdType.MESH
+        )
+    pl.semaphore_wait(barrier, count)
+
+    def order(c):
+        return levels if c % 2 == 0 else (levels[1], levels[0]) + levels[2:]
+
+    def span(c, level):
+        low, size = 0, rows
+        for bit in order(c)[:level]:
+            size = size // 2
+            low = low + lax.rem(me // (1 << bit), 2) * size
+        return low, size
+
+    def remote(c, stage, src, dst, bit):
+        return pltpu.make_async_remote_copy(
+            src_ref=src, dst_ref=dst,
+            send_sem=send_sem.at[c, stage], recv_sem=recv_sem.at[c, stage],
+            device_id={"row": flip(me, bit)}, device_id_type=pl.DeviceIdType.MESH,
+        )
+
+    flying = {}
+
+    def start(c, stage):
+        at = pl.ds(c * chunk, chunk)
+        if stage < count:
+            level, bit = stage, order(c)[stage]
+            low, size = span(c, level)
+            half = size // 2
+            theirs = low + (1 - lax.rem(me // (1 << bit), 2)) * half
+            src = (part_ref if level == 0 else acc).at[pl.ds(pl.multiple_of(theirs, 16), half), at]
+            dst = land.at[pl.ds(rows - size, half), at]
+        else:
+            level = 2 * count - 1 - stage
+            bit = order(c)[level]
+            low, size = span(c, level + 1)
+            src = out_ref.at[pl.ds(pl.multiple_of(low, 16), size), at]
+            dst = src
+        flying[c, stage] = remote(c, stage, src, dst, bit)
+        flying[c, stage].start()
+
+    def finish(c, stage):
+        flying[c, stage].wait()
+        if stage < count:
+            at = pl.ds(c * chunk, chunk)
+            low, size = span(c, stage + 1)
+            here = pl.ds(pl.multiple_of(low, 16), size)
+            mine = (part_ref if stage == 0 else acc)[here, at].astype(jnp.float32)
+            got = land[pl.ds(rows - 2 * size, size), at].astype(jnp.float32)
+            total = (mine + got).astype(jnp.bfloat16)
+            if stage == count - 1:
+                out_ref[here, at] = total
+            else:
+                acc[here, at] = total
+
+    ahead = 4
+    for c in range(min(ahead, chunks)):
+        start(c, 0)
+    for step in range(2 * count + (chunks - 1) // 2):
+        for c in range(chunks):
+            stage = step - c // 2
+            if 0 <= stage < 2 * count:
+                finish(c, stage)
+                if stage + 1 < 2 * count:
+                    start(c, stage + 1)
+                if stage == 0 and c + ahead < chunks:
+                    start(c + ahead, 0)
+
+
+def sum_over_rows(partial, row_count):
+    rows, cols = partial.shape
+    levels = tuple(range(row_count.bit_length() - 1))
+    count = len(levels)
+    chunk = 640 if cols % 640 == 0 else 128
+    chunks = cols // chunk
+    whole = pl.BlockSpec(memory_space=pltpu.VMEM)
+    return pl.pallas_call(
+        functools.partial(sum_kernel, levels, chunk),
+        out_shape=jax.ShapeDtypeStruct((rows, cols), jnp.bfloat16),
+        in_specs=[whole],
+        out_specs=whole,
+        scratch_shapes=[
+            pltpu.VMEM((rows, cols), jnp.bfloat16),
+            pltpu.VMEM((rows, cols), jnp.bfloat16),
+            pltpu.SemaphoreType.DMA((chunks, 2 * count)),
+            pltpu.SemaphoreType.DMA((chunks, 2 * count)),
+        ],
+        compiler_params=pltpu.CompilerParams(
+            collective_id=0, has_side_effects=True, vmem_limit_bytes=40 * 1024 * 1024
+        ),
+        cost_estimate=pl.CostEstimate(
+            flops=2 * rows * cols, bytes_accessed=200 * rows * cols, transcendentals=0
+        ),
+    )(partial)
+
+
 def on_device(
-    token_ids, set_lengths, live_counts, embed_table, position_table, norm_gain,
+    row_count, token_ids, set_lengths, live_counts, embed_table, position_table, norm_gain,
     w_query, w_key, w_value, w_out,
 ):
     sets, seq = token_ids.shape
@@ -95,11 +204,14 @@
         lax.dynamic_slice_in_dim(position_table, me * depth, depth, 1),
     ], axis=0).astype(jnp.float32)
     rows = (rows * lax.dynamic_slice_in_dim(norm_gain, me * depth, depth)).astype(jnp.bfloat16)
+    short = -rows.shape[0] % (16 * row_count)
+    if short:
+        rows = jnp.pad(rows, ((0, short), (0, 0)))
     partial = jnp.concatenate([
         jnp.dot(rows, w, preferred_element_type=jnp.float32).astype(jnp.bfloat16)
         for w in (w_query, w_key, w_value)
     ], axis=1)
-    table = lax.psum(partial, "row")
+    table = sum_over_rows(partial, row_count)
 
     out_full = lax.all_gather(w_out, "row", axis=1, tiled=True)
 
@@ -135,5 +247,5 @@
         P("row", "mp"), P("row", "mp"), P("row", "mp"), P("mp", "row"),
     )
     return jax.shard_map(
-        on_device, mesh=mesh, in_specs=in_specs, out_specs=P("row", None, "mp"), check_vma=False
-    )
+        functools.partial(on_device, mesh.shape["row"]), mesh=mesh, in_specs=in_specs, out_specs=P("row", None, "mp"), check_vma=False
+    )

time: 494 us -> 432 us (0.87)
  waiting for transfers between devices: 401 us -> 82.8 us
  Pallas kernels: 23.9 us -> 284 us
    pallas_call x0 -> x1, Pallas kernels: none -> 252 us  [sum_over_rows(): pl.pallas_call(functools.partial(sum_kernel, levels, chunk), out_shape=ja...]
    psum x1 -> x0, waiting for transfers between devices: 161 us -> none  [on_device(): table = lax.psum(partial, 'row')]
    all_gather x1, waiting for transfers between devices: 157 us -> 0.01 us  [on_device(): out_full = lax.all_gather(w_out, 'row', axis=1, tiled=True)]
    pallas_call x1, Pallas kernels: 23.9 us -> 31.5 us  [attend(): pl.pallas_call(functools.partial(attend_kernel, heads, vocab), out_shape=...]
  transfers between devices with their start and end apart: 3 -> 2, of which waited for: 3 -> 1; matrix products, arithmetic and copies ran while one was open for 3% -> 5% of each run, Pallas kernels for 5% -> 66%
where the time goes in v2:
time: 432 us; the launch traced here: 429 us
  Pallas kernels  284 us (66%)
  waiting for transfers between devices  82.8 us (19%)
  matrix products  35.8 us (8%)
  between operations  13.6 us (3%)
  other arithmetic  8.05 us (2%)
  local copies, waits for them, and re-layouts  5.45 us (1%)
    pallas_call x1, Pallas kernels, sum_over_rows(): pl.pallas_call(functools.partial(sum_kernel, levels, chunk), out_shape=ja...  252 us
    reduce_scatter x1, waiting for transfers between devices, on_device(): lax.psum_scatter(partial_out, 'mp', scatter_dimension=1, tiled=True)  82.1 us
    pallas_call x1, Pallas kernels, attend(): pl.pallas_call(functools.partial(attend_kernel, heads, vocab), out_shape=...  31.5 us
    dot_general x1, matrix products, on_device(): jnp.dot(mixed, out_full, preferred_element_type=jnp.float32)  19.8 us
    dot_general x1, matrix products, on_device(): picked = jnp.dot(pick, embed_table, preferred_element_type=jnp.float32)  11.7 us
  transfers between devices with their start and end apart: 2, of which 1 were waited for; matrix products, arithmetic and copies ran while one was open for 5% of the time, Pallas kernels for 66%

profile of v2, /device:TPU:0, one launch (start us, length us, event | category | flops | bytes accessed | tf_op | source)
XLA Modules:
  0.0 429.4 jit_solution(1055291143598424592)
XLA Ops:
  6.5 0.0 copy-start
  6.5 0.0 copy-start.4
  6.5 0.0 all-gather.2.cloned.1.call-start
  6.5 0.7 all-gather.2.cloned.1.call-update
  7.3 0.0 reduce-scatter.2.cloned.1.call-start
  7.3 1.6 convert_element_type.43
  8.9 0.0 copy-done.4
  8.9 0.0 copy-start.7
  8.9 11.7 %multiply_reduce_fusion = (f32[1024]{0:T(1024)S(1)}, bf16[1024,5120]{1,0:T(8,128)(2,1)}) fusion(f32[128,5120]{1,0:T(8,128)S(1)} %convert_element_type.43, bf16[512,5120]{1,0:T(8,128)(2,1)} %param.13, s32[1024]{0:T(1024)S(1)} %bitcast.18), kind=kOutput, calls=%fused_computation.2 | convolution fusion | flops 5395446784 | bytes 18358272 | tf_op jit(solution)/shard_map/dot_general | solution.py:219
  20.6 0.2 copy.12.inv_ref
  20.8 0.2 copy.11.ids_ref
  21.1 0.8 dynamic_slice.19
  21.9 0.0 copy-done.7
  21.9 0.5 dynamic_slice.15
  22.4 1.0 constant_dynamic-slice_fusion
  23.4 1.2 constant_dynamic-slice_fusion.1
  24.6 0.0 copy-done
  24.6 0.0 copy-start.5
  24.6 1.5 convolution_convert_fusion.1
  26.0 0.0 copy-done.5
  26.0 0.0 copy-start.6
  26.1 1.4 convolution_convert_fusion.2
  27.5 0.0 copy-done.6
  27.5 1.4 convolution_convert_fusion.3
  29.0 0.4 pad_maximum_fusion.part_ref
  29.3 0.0 copy-start.2
  29.4 252.1 %shard_map.100.table_ref = bf16[640,3840]{1,0:T(8,128)(2,1)S(1)} custom-call(bf16[640,3840]{1,0:T(8,128)(2,1)S(1)} %pad_maximum_fusion.part_ref), custom_call_target="tpu_custom_call" | custom-call | flops 4915200 | bytes 491520000 | tf_op jit(solution)/shard_map/pallas_call | solution.py:172
  281.5 0.5 fusion.7.live_ref
  282.1 0.0 copy-done.2
  282.1 31.5 %shard_map.101 = bf16[1024,1280]{1,0:T(8,128)(2,1)S(1)} custom-call(s32[8]{0:T(128)S(1)} %copy-done.2, s32[8]{0:T(128)S(1)} %fusion.7.live_ref, s32[8,128,1]{2,1,0:T(8,128)S(1)} %copy.11.ids_ref, f32[8,128,1]{2,1,0:T(8,128)S(1)} %copy.12.inv_ref, bf16[640,3840]{1,0:T(8,128)(2,1)S(1)} %shard_map.100.table_ref), custom_call_target="tpu_custom_call" | custom-call | flops 5033164800 | bytes 4915200 | tf_op jit(solution)/shard_map/pallas_call | solution.py:70
  313.5 0.0 copy-start.3
  313.5 1.5 copy-done.3
  315.0 0.0 all-gather.2.cloned.1.call-done
  315.0 19.8 %convolution_convert_fusion = bf16[1024,5120]{1,0:T(8,128)(2,1)} fusion(bf16[1024,1280]{1,0:T(8,128)(2,1)} %copy-done.3, bf16[1280,5120]{1,0:T(8,128)(2,1)} %all-gather.2.cloned.1.call-done), kind=kOutput, calls=%fused_computation.3 | convolution fusion | flops 13427015680 | bytes 26214400 | tf_op jit(solution)/shard_map/dot_general | solution.py:230
  334.9 0.0 reduce-scatter.2.cloned.1.call-update
  334.9 0.5 iota_compare_fusion.3
  335.4 0.1 fusion.3
  335.5 82.1 %reduce-scatter.2.cloned.1.call-done = bf16[1024,1280]{1,0:T(8,128)(2,1)} async-done(((bf16[1024,5120]{1,0:T(8,128)(2,1)}), bf16[1024,1280]{1,0:T(8,128)(2,1)}) %reduce-scatter.2.cloned.1.call-update) | async-done | bytes 2621456 | tf_op jit(solution)/shard_map/reduce_scatter | solution.py:231
  417.6 0.0 copy-start.1
  417.6 4.9 %select_convert_fusion = bf16[1024,1280]{1,0:T(8,128)(2,1)} fusion(bf16[1024,1280]{1,0:T(8,128)(2,1)} %reduce-scatter.2.cloned.1.call-done, bf16[1024,5120]{1,0:T(8,128)(2,1)} %get-tuple-element.6, s32[]{:T(128)S(6)} %select_n.16, pred[1024]{0:T(1024)(128)(4,1)S(1)} %fusion.3), kind=kLoop, calls=%fused_computation.4 | loop fusion | flops 6553600 | bytes 7865348 | tf_op jit(solution)/shard_map/convert_element_type | solution.py:240
  422.5 0.0 copy-done.1
  (1 shorter events, 0.0 us)
Async XLA Ops:
  6.5 18.0 %copy-start = (bf16[640,1280]{1,0:T(8,128)(2,1)S(1)}, bf16[640,1280]{1,0:T(8,128)(2,1)}, u32[]{:S(2)}) copy-start(bf16[640,1280]{1,0:T(8,128)(2,1)} %param.18) | copy-start | bytes 4915204
  6.5 2.4 copy-start.4
  6.5 308.5 %all-gather.2.cloned.1.call-start = ((), (), s32[]{:S(2)}) async-start(), calls=%async_computation.1 | async-start | bytes 14745600 | tf_op jit(solution)/shard_map/all_gather | solution.py:216
  7.3 410.3 %reduce-scatter.2.cloned.1.call-start = ((), (), s32[]{:S(2)}) async-start(), calls=%async_computation.2 | async-start | bytes 13107200 | tf_op jit(solution)/shard_map/reduce_scatter | solution.py:231
  8.9 13.0 %copy-start.7 = (s32[8]{0:T(128)S(1)}, s32[8]{0:T(128)}, u32[]{:S(2)}) copy-start(s32[8]{0:T(128)} %param.12) | copy-start | bytes 100
  24.6 1.5 copy-start.5
  26.0 1.5 copy-start.6
  29.3 252.7 %copy-start.2 = (s32[8]{0:T(128)S(1)}, s32[8]{0:T(128)}, u32[]{:S(2)}) copy-start(s32[8]{0:T(128)} %lengths_ref.1) | copy-start | bytes 100
  313.5 1.5 copy-start.3
  417.6 4.9 %copy-start.1 = (bf16[640,1280]{1,0:T(8,128)(2,1)S(1)}, bf16[640,1280]{1,0:T(8,128)(2,1)}, u32[]{:S(2)}) copy-start(bf16[640,1280]{1,0:T(8,128)(2,1)} %param.18) | copy-start | bytes 4915204
Sparse Core Ops, SparseCore 0:
  9.6 279.5 all-gather.1
  335.0 82.5 reduce-scatter.1

commit v3 on v2

--- a/solution.py
+++ b/solution.py
@@ -189,8 +189,151 @@
     )(partial)
 
 
+def bit_of(index, bit):
+    return lax.rem(index // (1 << bit), 2)
+
+
+class Scatter:
+    def __init__(self, part, count, mixed, weight, out, buf, land, send_sem, recv_sem):
+        self.part, self.count = part, count
+        self.mixed, self.weight, self.out = mixed, weight, out
+        self.buf, self.land = buf, land
+        self.send_sem, self.recv_sem = send_sem, recv_sem
+        self.chunks, self.half, self.rows, self.width = buf.shape
+        self.flying = {}
+
+    def product(self, c, mine, finish):
+        features = self.chunks * self.width
+        tile = min(256, self.rows)
+        first = bit_of(self.part, 0)
+        first = first if mine else 1 - first
+        for p in range(self.half):
+            block = first
+            for i in range(1, self.count):
+                block = block + (1 << i) * ((p >> (self.count - 1 - i)) & 1)
+            at = pl.multiple_of(block * features + c * self.width, 128)
+
+            @pl.loop(0, self.rows // tile)
+            def _(t):
+                here = pl.ds(pl.multiple_of(t * tile, tile), tile)
+                got = jnp.dot(
+                    self.mixed[here, :], self.weight[:, pl.ds(at, self.width)],
+                    preferred_element_type=jnp.float32,
+                )
+                if mine:
+                    got = got + self.land[c, p, here, :].astype(jnp.float32)
+                finish(c, p, here, got.astype(jnp.bfloat16))
+
+    def kept(self, level):
+        low, size = 0, self.half
+        for bit in range(1, level + 1):
+            size = size // 2
+            low = low + bit_of(self.part, bit) * size
+        return low, size
+
+    def start(self, c, level):
+        if level == 0:
+            def store(c, p, here, value):
+                self.buf[c, p, here, :] = value
+            self.product(c, False, store)
+            src, dst = self.buf.at[c], self.land.at[c, pl.ds(0, self.half)]
+        else:
+            low, size = self.kept(level - 1)
+            size = size // 2
+            theirs = low + (1 - bit_of(self.part, level)) * size
+            src = self.buf.at[c, pl.ds(theirs, size)]
+            dst = self.land.at[c, pl.ds(2 * self.half - 2 * size, size)]
+        copy = pltpu.make_async_remote_copy(
+            src_ref=src, dst_ref=dst,
+            send_sem=self.send_sem.at[c, level], recv_sem=self.recv_sem.at[c, level],
+            device_id={"mp": flip(self.part, level)}, device_id_type=pl.DeviceIdType.MESH,
+        )
+        copy.start()
+        self.flying[c, level] = copy
+
+    def finish(self, c, level):
+        self.flying[c, level].wait()
+        last = level == self.count - 1
+        columns = pl.ds(c * self.width, self.width)
+        if level == 0:
+            def store(c, p, here, value):
+                if last:
+                    self.out[here, columns] = value
+                else:
+                    self.buf[c, p, here, :] = value
+            self.product(c, True, store)
+        else:
+            low, size = self.kept(level)
+            tile = min(256, self.rows)
+            for k in range(size):
+                @pl.loop(0, self.rows // tile)
+                def _(t):
+                    here = pl.ds(pl.multiple_of(t * tile, tile), tile)
+                    got = self.land[c, 2 * self.half - 2 * size + k, here, :].astype(jnp.float32)
+                    value = (self.buf[c, low + k, here, :].astype(jnp.float32) + got).astype(jnp.bfloat16)
+                    if last:
+                        self.out[here, columns] = value
+                    else:
+                        self.buf[c, low + k, here, :] = value
+
+    def advance(self, step):
+        if step < self.chunks:
+            self.start(step, 0)
+        for level in range(self.count):
+            c = step - 1 - level
+            if 0 <= c < self.chunks:
+                self.finish(c, level)
+                if level + 1 < self.count:
+                    self.start(c, level + 1)
+
+    def steps(self):
+        return self.chunks + self.count
+
+
+def scatter_kernel(count, mixed_ref, weight_ref, out_ref, buf, land, send_sem, recv_sem):
+    part = lax.axis_index("mp")
+    barrier = pltpu.get_barrier_semaphore()
+    for bit in range(count):
+        pl.semaphore_signal(
+            barrier, inc=1, device_id={"mp": flip(part, bit)}, device_id_type=pl.DeviceIdType.MESH
+        )
+    pl.semaphore_wait(barrier, count)
+    work = Scatter(part, count, mixed_ref, weight_ref, out_ref, buf, land, send_sem, recv_sem)
+    for step in range(work.steps()):
+        work.advance(step)
+
+
+def project_out(mixed, weight, part_count):
+    rows = mixed.shape[0]
+    features = weight.shape[1] // part_count
+    count = part_count.bit_length() - 1
+    chunks = 5 if features % 640 == 0 else 1
+    width = features // chunks
+    half = part_count // 2
+    whole = pl.BlockSpec(memory_space=pltpu.VMEM)
+    return pl.pallas_call(
+        functools.partial(scatter_kernel, count),
+        out_shape=jax.ShapeDtypeStruct((rows, features), jnp.bfloat16),
+        in_specs=[whole, whole],
+        out_specs=whole,
+        scratch_shapes=[
+            pltpu.VMEM((chunks, half, rows, width), jnp.bfloat16),
+            pltpu.VMEM((chunks, 2 * half - 1, rows, width), jnp.bfloat16),
+            pltpu.SemaphoreType.DMA((chunks, count)),
+            pltpu.SemaphoreType.DMA((chunks, count)),
+        ],
+        compiler_params=pltpu.CompilerParams(
+            collective_id=1, has_side_effects=True, vmem_limit_bytes=56 * 1024 * 1024
+        ),
+        cost_estimate=pl.CostEstimate(
+            flops=2 * rows * mixed.shape[1] * weight.shape[1],
+            bytes_accessed=2 * weight.size, transcendentals=0,
+        ),
+    )(mixed, weight)
+
+
 def on_device(
-    row_count, token_ids, set_lengths, live_counts, embed_table, position_table, norm_gain,
+    row_count, part_count, token_ids, set_lengths, live_counts, embed_table, position_table, norm_gain,
     w_query, w_key, w_value, w_out,
 ):
     sets, seq = token_ids.shape
@@ -227,10 +370,7 @@
     mixed = attend(
         token_ids, set_lengths, live.astype(jnp.int32), inv, table, heads, vocab
     )
-    partial_out = jnp.dot(mixed, out_full, preferred_element_type=jnp.float32).astype(jnp.bfloat16)
-    summed = lax.psum_scatter(
-        partial_out, "mp", scatter_dimension=1, tiled=True
-    ).astype(jnp.float32)
+    summed = project_out(mixed, out_full, part_count).astype(jnp.float32)
     features = summed.shape[1]
     residual = lax.dynamic_slice_in_dim(
         stored.reshape(sets * seq, d), part * features, features, 1
@@ -247,5 +387,5 @@
         P("row", "mp"), P("row", "mp"), P("row", "mp"), P("mp", "row"),
     )
     return jax.shard_map(
-        functools.partial(on_device, mesh.shape["row"]), mesh=mesh, in_specs=in_specs, out_specs=P("row", None, "mp"), check_vma=False
+        functools.partial(on_device, mesh.shape["row"], mesh.shape["mp"]), mesh=mesh, in_specs=in_specs, out_specs=P("row", None, "mp"), check_vma=False
     )

time: 432 us -> 402 us (0.931)
  the two profiles are of different devices: /device:TPU:0 before, /device:TPU:16 now
where the time goes in v3:
time: 402 us; the launch traced here: 398 us
  Pallas kernels  355 us (88%)
  matrix products  16.1 us (4%)
  between operations  13.6 us (3%)
  other arithmetic  6.18 us (2%)
  local copies, waits for them, and re-layouts  6.16 us (2%)
    pallas_call x1, Pallas kernels, sum_over_rows(): pl.pallas_call(functools.partial(sum_kernel, levels, chunk), out_shape=ja...  252 us
    pallas_call x1, Pallas kernels, project_out(): pl.pallas_call(functools.partial(scatter_kernel, count), out_shape=jax.Sh...  75.1 us
    pallas_call x1, Pallas kernels, attend(): pl.pallas_call(functools.partial(attend_kernel, heads, vocab), out_shape=...  27.6 us
    dot_general x1, matrix products, on_device(): picked = jnp.dot(pick, embed_table, preferred_element_type=jnp.float32)  11.8 us
  transfers between devices with their start and end apart: 1, of which 0 were waited for; matrix products, arithmetic and copies ran while one was open for 5% of the time, Pallas kernels for 70%

profile of v3, /device:TPU:16, one launch (start us, length us, event | category | flops | bytes accessed | tf_op | source)
XLA Modules:
  0.0 397.7 jit_solution(12188597449152672680)
XLA Ops:
  6.5 0.0 copy-start
  6.5 0.0 copy-start.3
  6.5 0.0 all-gather.2.cloned.1.call-start
  6.5 0.7 all-gather.2.cloned.1.call-update
  7.3 0.0 copy-start.4
  7.3 0.7 copy-done.3
  8.0 0.2 convert_element_type.40
  8.2 0.0 copy-done.4
  8.2 0.0 copy-start.7
  8.3 11.8 %multiply_reduce_fusion = (f32[1024]{0:T(1024)S(1)}, bf16[1024,5120]{1,0:T(8,128)(2,1)}) fusion(f32[128,5120]{1,0:T(8,128)S(1)} %convert_element_type.40, bf16[512,5120]{1,0:T(8,128)(2,1)} %param.13, s32[1024]{0:T(1024)S(1)} %bitcast.16), kind=kOutput, calls=%fused_computation.2 | convolution fusion | flops 5395446784 | bytes 18358272 | tf_op jit(solution)/shard_map/dot_general | solution.py:362
  20.0 0.2 copy.12.inv_ref
  20.3 0.2 copy.11.ids_ref
  20.5 0.8 dynamic_slice.19
  21.3 0.0 copy-done.7
  21.3 0.6 dynamic_slice.15
  21.9 1.0 constant_dynamic-slice_fusion
  22.9 1.2 constant_dynamic-slice_fusion.1
  24.0 0.0 copy-done
  24.0 0.0 copy-start.5
  24.0 1.5 convolution_convert_fusion
  25.5 0.0 copy-done.5
  25.5 0.0 copy-start.6
  25.5 1.4 convolution_convert_fusion.1
  27.0 0.0 copy-done.6
  27.0 1.4 convolution_convert_fusion.2
  28.4 0.4 pad_maximum_fusion.part_ref
  28.8 0.0 copy-start.1
  28.8 252.1 %shard_map.100.table_ref = bf16[640,3840]{1,0:T(8,128)(2,1)S(1)} custom-call(bf16[640,3840]{1,0:T(8,128)(2,1)S(1)} %pad_maximum_fusion.part_ref), custom_call_target="tpu_custom_call" | custom-call | flops 4915200 | bytes 491520000 | tf_op jit(solution)/shard_map/pallas_call | solution.py:172
  280.9 0.7 iota_compare_fusion.3
  281.6 0.0 copy-done.1
  281.6 0.1 fusion.3
  281.7 27.6 %shard_map.101.mixed_ref = bf16[1024,1280]{1,0:T(8,128)(2,1)S(1)} custom-call(s32[8]{0:T(128)S(1)} %copy-done.1, s32[8]{0:T(128)S(1)} %get-tuple-element.8.live_ref, s32[8,128,1]{2,1,0:T(8,128)S(1)} %copy.11.ids_ref, f32[8,128,1]{2,1,0:T(8,128)S(1)} %copy.12.inv_ref, bf16[640,3840]{1,0:T(8,128)(2,1)S(1)} %shard_map.100.table_ref), custom_call_target="tpu_custom_call" | custom-call | flops 5033164800 | bytes 4915200 | tf_op jit(solution)/shard_map/pallas_call | solution.py:70
  309.3 0.0 copy-start.2
  309.3 1.5 copy-done.2
  310.8 0.0 all-gather.2.cloned.1.call-done.weight_ref
  310.8 75.1 %shard_map.102 = bf16[1024,1280]{1,0:T(8,128)(2,1)} custom-call(bf16[1024,1280]{1,0:T(8,128)(2,1)} %copy-done.2, bf16[1280,5120]{1,0:T(8,128)(2,1)} %all-gather.2.cloned.1.call-done.weight_ref), custom_call_target="tpu_custom_call" | custom-call | flops 13421772800 | bytes 13107200 | tf_op jit(solution)/shard_map/pallas_call | solution.py:314
  386.0 4.8 %select_convert_fusion = bf16[1024,1280]{1,0:T(8,128)(2,1)} fusion(bf16[1024,1280]{1,0:T(8,128)(2,1)} %shard_map.102, bf16[1024,5120]{1,0:T(8,128)(2,1)} %get-tuple-element.6, s32[]{:T(128)S(6)} %select_n.16, pred[1024]{0:T(1024)(128)(4,1)S(1)} %fusion.3), kind=kLoop, calls=%fused_computation.3 | loop fusion | flops 6553600 | bytes 7865348 | tf_op jit(solution)/shard_map/convert_element_type | solution.py:380
  (1 shorter events, 0.0 us)
Async XLA Ops:
  6.5 17.5 %copy-start = (bf16[640,1280]{1,0:T(8,128)(2,1)S(1)}, bf16[640,1280]{1,0:T(8,128)(2,1)}, u32[]{:S(2)}) copy-start(bf16[640,1280]{1,0:T(8,128)(2,1)} %param.18) | copy-start | bytes 4915204
  6.5 1.4 copy-start.3
  6.5 304.3 %all-gather.2.cloned.1.call-start = ((), (), s32[]{:S(2)}) async-start(), calls=%async_computation | async-start | bytes 14745600 | tf_op jit(solution)/shard_map/all_gather | solution.py:359
  7.3 1.0 copy-start.4
  8.2 13.1 %copy-start.7 = (s32[8]{0:T(128)S(1)}, s32[8]{0:T(128)}, u32[]{:S(2)}) copy-start(s32[8]{0:T(128)} %param.12) | copy-start | bytes 100
  24.0 1.5 copy-start.5
  25.5 1.5 copy-start.6
  28.8 252.8 %copy-start.1 = (s32[8]{0:T(128)S(1)}, s32[8]{0:T(128)}, u32[]{:S(2)}) copy-start(s32[8]{0:T(128)} %lengths_ref.1) | copy-start | bytes 100
  309.3 1.5 copy-start.2
Sparse Core Ops, SparseCore 0:
  9.6 278.9 all-gather.1

commit v4 on v3

--- a/solution.py
+++ b/solution.py
@@ -9,6 +9,37 @@
 DH = 128
 
 
+def attend_set(heads, vocab, ids, inv, masked, table_ref, store):
+    seq = ids.shape[0]
+    width = heads * DH
+    cols = lax.broadcasted_iota(jnp.int32, (seq, vocab + seq), 1)
+    rows = lax.broadcasted_iota(jnp.int32, (seq, vocab + seq), 0)
+    pick = jnp.where((cols == ids) | (cols == rows + vocab), 1.0, 0.0).astype(jnp.bfloat16)
+    pieces = {}
+    for part in range(3):
+        at = 0
+        while at < width:
+            step = min(2 * DH, width - at)
+            got = jnp.dot(
+                pick, table_ref[:vocab + seq, part * width + at:part * width + at + step],
+                preferred_element_type=jnp.float32,
+            )
+            got = (got * inv).astype(jnp.bfloat16)
+            for k in range(step // DH):
+                pieces[part, at // DH + k] = got[:, k * DH:(k + 1) * DH]
+            at += step
+    for h in range(heads):
+        q, k, v = pieces[0, h], pieces[1, h], pieces[2, h]
+        scores = lax.dot_general(
+            q, k, (((1,), (1,)), ((), ())), preferred_element_type=jnp.float32
+        ) * DH ** (-0.5)
+        scores = jnp.where(masked, -1e30, scores)
+        expo = jnp.exp(scores - jnp.max(scores, axis=-1, keepdims=True))
+        weights = (expo / jnp.sum(expo, axis=-1, keepdims=True)).astype(jnp.bfloat16)
+        mixed = jnp.dot(weights, v, preferred_element_type=jnp.float32)
+        store(h, mixed.astype(jnp.bfloat16))
+
+
 def attend_kernel(heads, vocab, lengths_ref, live_ref, ids_ref, inv_ref, table_ref, out_ref):
     s = pl.program_id(0)
     seq = out_ref.shape[0]
@@ -21,37 +52,15 @@
 
     @pl.when(live_ref[s] != 0)
     def _():
-        ids = ids_ref[...].reshape(seq, 1)
-        cols = lax.broadcasted_iota(jnp.int32, (seq, vocab + seq), 1)
-        rows = lax.broadcasted_iota(jnp.int32, (seq, vocab + seq), 0)
-        pick = jnp.where((cols == ids) | (cols == rows + vocab), 1.0, 0.0).astype(jnp.bfloat16)
-        inv = inv_ref[...].reshape(seq, 1)
         masked = lax.broadcasted_iota(jnp.int32, (seq, seq), 1) >= length
 
-
-        pieces = {}
-        for part in range(3):
-            at = 0
-            while at < width:
-                step = min(2 * DH, width - at)
-                got = jnp.dot(
-                    pick, table_ref[:vocab + seq, part * width + at:part * width + at + step],
-                    preferred_element_type=jnp.float32,
-                )
-                got = (got * inv).astype(jnp.bfloat16)
-                for k in range(step // DH):
-                    pieces[part, at // DH + k] = got[:, k * DH:(k + 1) * DH]
-                at += step
-        for h in range(heads):
-            q, k, v = pieces[0, h], pieces[1, h], pieces[2, h]
-            scores = lax.dot_general(
-                q, k, (((1,), (1,)), ((), ())), preferred_element_type=jnp.float32
-            ) * DH ** (-0.5)
-            scores = jnp.where(masked, -1e30, scores)
-            expo = jnp.exp(scores - jnp.max(scores, axis=-1, keepdims=True))
-            weights = (expo / jnp.sum(expo, axis=-1, keepdims=True)).astype(jnp.bfloat16)
-            mixed = jnp.dot(weights, v, preferred_element_type=jnp.float32)
-            out_ref[:, h * DH:(h + 1) * DH] = mixed.astype(jnp.bfloat16)
+        def store(h, value):
+            out_ref[:, h * DH:(h + 1) * DH] = value
+
+        attend_set(
+            heads, vocab, ids_ref[...].reshape(seq, 1), inv_ref[...].reshape(seq, 1), masked,
+            table_ref, store,
+        )
 
 
 def attend(ids, lengths, live, inv, table, heads, vocab):
@@ -80,86 +89,106 @@
     )(lengths, live, ids[..., None], inv[..., None], table)
 
 
+def bit_of(index, bit):
+    return lax.rem(index // (1 << bit), 2)
+
+
 def flip(me, bit):
     return me + (1 - 2 * (lax.rem(me // (1 << bit), 2))) * (1 << bit)
 
 
-def sum_kernel(levels, chunk, part_ref, out_ref, land, acc, send_sem, recv_sem):
-    me = lax.axis_index("row")
-    rows, cols = part_ref.shape
-    chunks = cols // chunk
-    count = len(levels)
-
+class RowSum:
+    def __init__(self, me, levels, chunk, part, out, land, acc, send_sem, recv_sem):
+        self.me, self.levels, self.chunk = me, levels, chunk
+        self.part, self.out, self.land, self.acc = part, out, land, acc
+        self.send_sem, self.recv_sem = send_sem, recv_sem
+        self.rows, cols = part.shape
+        self.chunks, self.count = cols // chunk, len(levels)
+        self.flying = {}
+
+    def order(self, c):
+        levels = self.levels
+        return levels if c % 2 == 0 else (levels[1], levels[0]) + levels[2:]
+
+    def span(self, c, level):
+        low, size = 0, self.rows
+        for bit in self.order(c)[:level]:
+            size = size // 2
+            low = low + bit_of(self.me, bit) * size
+        return low, size
+
+    def start(self, c, stage):
+        at = pl.ds(c * self.chunk, self.chunk)
+        if stage < self.count:
+            level, bit = stage, self.order(c)[stage]
+            low, size = self.span(c, level)
+            half = size // 2
+            theirs = low + (1 - bit_of(self.me, bit)) * half
+            held = self.part if level == 0 else self.acc
+            src = held.at[pl.ds(pl.multiple_of(theirs, 16), half), at]
+            dst = self.land.at[pl.ds(self.rows - size, half), at]
+        else:
+            level = 2 * self.count - 1 - stage
+            bit = self.order(c)[level]
+            low, size = self.span(c, level + 1)
+            src = self.out.at[pl.ds(pl.multiple_of(low, 16), size), at]
+            dst = src
+        copy = pltpu.make_async_remote_copy(
+            src_ref=src, dst_ref=dst,
+            send_sem=self.send_sem.at[c, stage], recv_sem=self.recv_sem.at[c, stage],
+            device_id={"row": flip(self.me, bit)}, device_id_type=pl.DeviceIdType.MESH,
+        )
+        copy.start()
+        self.flying[c, stage] = copy
+
+    def finish(self, c, stage):
+        self.flying[c, stage].wait()
+        if stage < self.count:
+            at = pl.ds(c * self.chunk, self.chunk)
+            low, size = self.span(c, stage + 1)
+            here = pl.ds(pl.multiple_of(low, 16), size)
+            mine = (self.part if stage == 0 else self.acc)[here, at].astype(jnp.float32)
+            got = self.land[pl.ds(self.rows - 2 * size, size), at].astype(jnp.float32)
+            total = (mine + got).astype(jnp.bfloat16)
+            if stage == self.count - 1:
+                self.out[here, at] = total
+            else:
+                self.acc[here, at] = total
+
+    def run(self, beside=None):
+        stages, ahead = 2 * self.count, 4
+        for c in range(min(ahead, self.chunks)):
+            self.start(c, 0)
+        for step in range(stages + (self.chunks - 1) // 2):
+            if beside is not None and step == self.count:
+                beside()
+            for c in range(self.chunks):
+                stage = step - c // 2
+                if 0 <= stage < stages:
+                    self.finish(c, stage)
+                    if stage + 1 < stages:
+                        self.start(c, stage + 1)
+                    if stage == 0 and c + ahead < self.chunks:
+                        self.start(c + ahead, 0)
+
+
+def greet(me, count, part, part_count):
     barrier = pltpu.get_barrier_semaphore()
     for bit in range(count):
         pl.semaphore_signal(
             barrier, inc=1, device_id={"row": flip(me, bit)}, device_id_type=pl.DeviceIdType.MESH
         )
-    pl.semaphore_wait(barrier, count)
-
-    def order(c):
-        return levels if c % 2 == 0 else (levels[1], levels[0]) + levels[2:]
-
-    def span(c, level):
-        low, size = 0, rows
-        for bit in order(c)[:level]:
-            size = size // 2
-            low = low + lax.rem(me // (1 << bit), 2) * size
-        return low, size
-
-    def remote(c, stage, src, dst, bit):
-        return pltpu.make_async_remote_copy(
-            src_ref=src, dst_ref=dst,
-            send_sem=send_sem.at[c, stage], recv_sem=recv_sem.at[c, stage],
-            device_id={"row": flip(me, bit)}, device_id_type=pl.DeviceIdType.MESH,
-        )
-
-    flying = {}
-
-    def start(c, stage):
-        at = pl.ds(c * chunk, chunk)
-        if stage < count:
-            level, bit = stage, order(c)[stage]
-            low, size = span(c, level)
-            half = size // 2
-            theirs = low + (1 - lax.rem(me // (1 << bit), 2)) * half
-            src = (part_ref if level == 0 else acc).at[pl.ds(pl.multiple_of(theirs, 16), half), at]
-            dst = land.at[pl.ds(rows - size, half), at]
-        else:
-            level = 2 * count - 1 - stage
-            bit = order(c)[level]
-            low, size = span(c, level + 1)
-            src = out_ref.at[pl.ds(pl.multiple_of(low, 16), size), at]
-            dst = src
-        flying[c, stage] = remote(c, stage, src, dst, bit)
-        flying[c, stage].start()
-
-    def finish(c, stage):
-        flying[c, stage].wait()
-        if stage < count:
-            at = pl.ds(c * chunk, chunk)
-            low, size = span(c, stage + 1)
-            here = pl.ds(pl.multiple_of(low, 16), size)
-            mine = (part_ref if stage == 0 else acc)[here, at].astype(jnp.float32)
-            got = land[pl.ds(rows - 2 * size, size), at].astype(jnp.float32)
-            total = (mine + got).astype(jnp.bfloat16)
-            if stage == count - 1:
-                out_ref[here, at] = total
-            else:
-                acc[here, at] = total
-
-    ahead = 4
-    for c in range(min(ahead, chunks)):
-        start(c, 0)
-    for step in range(2 * count + (chunks - 1) // 2):
-        for c in range(chunks):
-            stage = step - c // 2
-            if 0 <= stage < 2 * count:
-                finish(c, stage)
-                if stage + 1 < 2 * count:
-                    start(c, stage + 1)
-                if stage == 0 and c + ahead < chunks:
-                    start(c + ahead, 0)
+    for bit in range(part_count):
+        pl.semaphore_signal(
+            barrier, inc=1, device_id={"mp": flip(part, bit)}, device_id_type=pl.DeviceIdType.MESH
+        )
+    pl.semaphore_wait(barrier, count + part_count)
+
+
+def sum_kernel(levels, chunk, part_ref, out_ref, land, acc, send_sem, recv_sem):
+    me = lax.axis_index("row")
+    greet(me, len(levels), 0, 0)
+    RowSum(me, levels, chunk, part_ref, out_ref, land, acc, send_sem, recv_sem).run()
 
 
 def sum_over_rows(partial, row_count):
@@ -189,10 +218,6 @@
     )(partial)
 
 
-def bit_of(index, bit):
-    return lax.rem(index // (1 << bit), 2)
-
-
 class Scatter:
     def __init__(self, part, count, mixed, weight, out, buf, land, send_sem, recv_sem):
         self.part, self.count = part, count
@@ -202,8 +227,14 @@
         self.chunks, self.half, self.rows, self.width = buf.shape
         self.flying = {}
 
+    def columns(self, c, block):
+        at = pl.multiple_of(block * self.chunks * self.width + c * self.width, 128)
+        return self.weight[:, pl.ds(at, self.width)]
+
+    def store(self, c, here, value):
+        self.out[here, pl.ds(c * self.width, self.width)] = value
+
     def product(self, c, mine, finish):
-        features = self.chunks * self.width
         tile = min(256, self.rows)
         first = bit_of(self.part, 0)
         first = first if mine else 1 - first
@@ -211,13 +242,13 @@
             block = first
             for i in range(1, self.count):
                 block = block + (1 << i) * ((p >> (self.count - 1 - i)) & 1)
-            at = pl.multiple_of(block * features + c * self.width, 128)
+            load = functools.partial(self.columns, c, block)
 
             @pl.loop(0, self.rows // tile)
             def _(t):
                 here = pl.ds(pl.multiple_of(t * tile, tile), tile)
                 got = jnp.dot(
-                    self.mixed[here, :], self.weight[:, pl.ds(at, self.width)],
+                    self.mixed[here, :], load(),
                     preferred_element_type=jnp.float32,
                 )
                 if mine:
@@ -254,11 +285,10 @@
     def finish(self, c, level):
         self.flying[c, level].wait()
         last = level == self.count - 1
-        columns = pl.ds(c * self.width, self.width)
         if level == 0:
             def store(c, p, here, value):
                 if last:
-                    self.out[here, columns] = value
+                    self.store(c, here, value)
                 else:
                     self.buf[c, p, here, :] = value
             self.product(c, True, store)
@@ -272,7 +302,7 @@
                     got = self.land[c, 2 * self.half - 2 * size + k, here, :].astype(jnp.float32)
                     value = (self.buf[c, low + k, here, :].astype(jnp.float32) + got).astype(jnp.bfloat16)
                     if last:
-                        self.out[here, columns] = value
+                        self.store(c, here, value)
                     else:
                         self.buf[c, low + k, here, :] = value
 
@@ -332,6 +362,145 @@
     )(mixed, weight)
 
 
+class Gather:
+    def __init__(self, me, levels, held, send_sem, recv_sem):
+        self.me, self.levels, self.held = me, levels, held
+        self.send_sem, self.recv_sem = send_sem, recv_sem
+        self.flying = {}
+
+    def order(self, c):
+        order = tuple(reversed(self.levels))
+        return order if c % 2 == 0 else order[:-2] + (order[-1], order[-2])
+
+    def start(self, c, level):
+        order = self.order(c)
+        to = flip(self.me, order[level])
+        for i in range(1 << level):
+            block = self.me
+            for k in range(level):
+                if (i >> k) & 1:
+                    block = flip(block, order[k])
+            slot = (1 << level) - 1 + i
+            copy = pltpu.make_async_remote_copy(
+                src_ref=self.held.at[c, block], dst_ref=self.held.at[c, block],
+                send_sem=self.send_sem.at[c, slot], recv_sem=self.recv_sem.at[c, slot],
+                device_id={"row": to}, device_id_type=pl.DeviceIdType.MESH,
+            )
+            copy.start()
+            self.flying[c, slot] = copy
+
+    def finish(self, c, level):
+        for i in range(1 << level):
+            self.flying[c, (1 << level) - 1 + i].wait()
+
+
+class BlockScatter(Scatter):
+    def columns(self, c, block):
+        per = self.width // self.weight.shape[-1]
+        return jnp.concatenate([self.weight[c, block * per + q] for q in range(per)], axis=1)
+
+    def store(self, c, here, value):
+        piece = self.weight.shape[-1]
+        for q in range(self.width // piece):
+            at = q * self.chunks * piece + c * piece
+            self.out[here, pl.ds(at, piece)] = value[:, q * piece:(q + 1) * piece]
+
+
+def whole_kernel(
+    levels, count, heads, vocab, chunk, part_ref, w_ref, ids_ref, inv_ref, valid_ref, out_ref,
+    table, land, acc, held, mixed, buf, land_out, row_sems, held_sems, out_sems,
+):
+    me, part = lax.axis_index("row"), lax.axis_index("mp")
+    sets, seq, _ = ids_ref.shape
+    chunks, _, _, piece = held.shape
+    greet(me, len(levels), part, count)
+    for c in range(chunks):
+        held[c, me] = w_ref[:, c * piece:(c + 1) * piece]
+    gather = Gather(me, levels, held, held_sems.at[0], held_sems.at[1])
+    total = RowSum(me, levels, chunk, part_ref, table, land, acc, row_sems.at[0], row_sems.at[1])
+    scatter = BlockScatter(part, count, mixed, held, out_ref, buf, land_out, out_sems.at[0], out_sems.at[1])
+    last = len(levels) - 1
+
+    def first():
+        for c in range(chunks):
+            gather.start(c, 0)
+
+    total.run(first)
+    for level in range(last - 1):
+        for c in range(chunks):
+            gather.finish(c, level)
+            gather.start(c, level + 1)
+    pairs = [tuple(range(c, min(c + 2, chunks))) for c in range(0, chunks, 2)]
+
+    def move(pair, level):
+        for c in pair:
+            gather.finish(c, level)
+            gather.start(c, level + 1)
+
+    move(pairs[0], last - 1)
+
+    @pl.loop(0, sets)
+    def _(s):
+        masked = jnp.broadcast_to(valid_ref[s], (seq, seq)) == 0
+        here = pl.ds(pl.multiple_of(s * seq, seq), seq)
+
+        def store(h, value):
+            mixed[here, h * DH:(h + 1) * DH] = value
+
+        attend_set(heads, vocab, ids_ref[s], inv_ref[s], masked, table, store)
+
+    for n, pair in enumerate(pairs):
+        if n + 1 < len(pairs):
+            move(pairs[n + 1], last - 1)
+        for c in pair:
+            gather.finish(c, last)
+            scatter.advance(c)
+    for step in range(chunks, scatter.steps()):
+        scatter.advance(step)
+
+
+def run_whole(partial, w_out, ids, inv, valid, row_count, part_count, heads, vocab):
+    rows, cols = partial.shape
+    sets, seq = ids.shape
+    depth, own = w_out.shape
+    piece = 128
+    chunks = own // piece
+    features = own * row_count // part_count
+    levels = tuple(range(row_count.bit_length() - 1))
+    count = part_count.bit_length() - 1
+    half, width = part_count // 2, features // chunks
+    chunk = 640
+    pieces = cols // chunk
+    flat = sets * seq
+    vmem = pl.BlockSpec(memory_space=pltpu.VMEM)
+    dma = pltpu.SemaphoreType.DMA
+    return pl.pallas_call(
+        functools.partial(whole_kernel, levels, count, heads, vocab, chunk),
+        out_shape=jax.ShapeDtypeStruct((flat, features), jnp.bfloat16),
+        in_specs=[vmem] * 5,
+        out_specs=vmem,
+        scratch_shapes=[
+            pltpu.VMEM((rows, cols), jnp.bfloat16),
+            pltpu.VMEM((rows, cols), jnp.bfloat16),
+            pltpu.VMEM((rows, cols), jnp.bfloat16),
+            pltpu.VMEM((chunks, row_count, depth, piece), jnp.bfloat16),
+            pltpu.VMEM((flat, heads * DH), jnp.bfloat16),
+            pltpu.VMEM((chunks, half, flat, width), jnp.bfloat16),
+            pltpu.VMEM((chunks, 2 * half - 1, flat, width), jnp.bfloat16),
+            dma((2, pieces, 2 * len(levels))),
+            dma((2, chunks, row_count - 1)),
+            dma((2, chunks, count)),
+        ],
+        compiler_params=pltpu.CompilerParams(
+            collective_id=2, has_side_effects=True, vmem_limit_bytes=60 * 1024 * 1024
+        ),
+        cost_estimate=pl.CostEstimate(
+            flops=2 * flat * depth * own * row_count, bytes_accessed=2 * flat * depth * 20,
+            transcendentals=0,
+        ),
+    )(partial, w_out, ids[..., None], inv[..., None], valid[:, None, :])
+
+
 def on_device(
     row_count, part_count, token_ids, set_lengths, live_counts, embed_table, position_table, norm_gain,
     w_query, w_key, w_value, w_out,
@@ -354,9 +523,6 @@
         jnp.dot(rows, w, preferred_element_type=jnp.float32).astype(jnp.bfloat16)
         for w in (w_query, w_key, w_value)
     ], axis=1)
-    table = sum_over_rows(partial, row_count)
-
-    out_full = lax.all_gather(w_out, "row", axis=1, tiled=True)
 
     pick = (token_ids.reshape(-1, 1) == jnp.arange(vocab)[None]).astype(jnp.bfloat16)
     picked = jnp.dot(pick, embed_table, preferred_element_type=jnp.float32)
@@ -367,15 +533,25 @@
     inv = lax.rsqrt(jnp.mean(widened * widened, axis=-1) + 1e-05)
 
     live = jnp.arange(sets) < live_counts[me]
-    mixed = attend(
-        token_ids, set_lengths, live.astype(jnp.int32), inv, table, heads, vocab
-    )
-    summed = project_out(mixed, out_full, part_count).astype(jnp.float32)
+    valid = jnp.arange(seq)[None, :] < set_lengths[:, None]
+    aligned = w_out.shape[1] % 128 == 0 and partial.shape[1] % 640 == 0
+    if aligned:
+        summed = run_whole(
+            partial, w_out, token_ids, inv, valid.astype(jnp.int32), row_count, part_count,
+            heads, vocab,
+        )
+    else:
+        table = sum_over_rows(partial, row_count)
+        out_full = lax.all_gather(w_out, "row", axis=1, tiled=True)
+        mixed = attend(
+            token_ids, set_lengths, live.astype(jnp.int32), inv, table, heads, vocab
+        )
+        summed = project_out(mixed, out_full, part_count)
+    summed = summed.astype(jnp.float32)
     features = summed.shape[1]
     residual = lax.dynamic_slice_in_dim(
         stored.reshape(sets * seq, d), part * features, features, 1
     ).astype(jnp.float32)
-    valid = jnp.arange(seq)[None, :] < set_lengths[:, None]
     keep = (live[:, None] & valid).reshape(-1, 1)
     output = jnp.where(keep, residual + summed, 0.0).astype(jnp.bfloat16)
     return output.reshape(sets, seq, features)

time: 402 us -> 361 us (0.90)
  the two profiles are of different devices: /device:TPU:16 before, /device:TPU:0 now
where the time goes in v4:
time: 361 us; the launch traced here: 360 us
  Pallas kernels  332 us (92%)
  matrix products  13.6 us (4%)
  other arithmetic  9.12 us (3%)
  local copies, waits for them, and re-layouts  6.09 us (2%)
    pallas_call x1, Pallas kernels, run_whole(): pl.pallas_call(functools.partial(whole_kernel, levels, count, heads, voca...  332 us
    dot_general x1, matrix products, on_device(): picked = jnp.dot(pick, embed_table, preferred_element_type=jnp.float32)  9.24 us

profile of v4, /device:TPU:0, one launch (start us, length us, event | category | flops | bytes accessed | tf_op | source)
XLA Modules:
  0.0 360.5 jit_solution(4865791391156318723)
XLA Ops:
  0.0 0.0 copy-start
  0.0 1.3 constant_dynamic-slice_fusion.1
  1.3 0.9 constant_dynamic-slice_fusion
  2.2 0.8 dynamic_slice.19
  3.0 0.0 copy-done
  3.0 0.0 copy-start.4
  3.0 1.4 convolution_convert_fusion.1
  4.5 0.0 copy-done.4
  4.5 0.0 copy-start.5
  4.5 1.5 convolution_convert_fusion.2
  5.9 0.0 copy-done.5
  5.9 0.0 slice-start
  6.0 1.5 convolution_convert_fusion
  7.4 0.0 copy-start.1
  7.4 0.0 slice-start.1
  7.4 2.6 pad_maximum_fusion.part_ref
  10.1 0.0 copy-done.1
  10.1 0.0 copy-start.2
  10.1 0.3 convert_element_type.47
  10.4 0.0 slice-done
  10.4 0.0 slice-done.1
  10.4 0.4 copy-done.2
  10.8 0.0 copy-start.3
  10.8 9.2 %multiply_reduce_fusion = (f32[1024]{0:T(1024)S(1)}, bf16[1024,5120]{1,0:T(8,128)(2,1)}) fusion(f32[128,5120]{1,0:T(8,128)S(1)} %convert_element_type.47, bf16[512,5120]{1,0:T(8,128)(2,1)S(1)} %bitcast.17, s32[1024]{0:T(1024)S(1)} %bitcast.18), kind=kOutput, calls=%fused_computation.2 | convolution fusion | flops 5395446784 | bytes 18358272 | tf_op jit(solution)/shard_map/dot_general | solution.py:528
  20.0 1.0 copy.12.inv_ref
  21.1 1.0 copy.11.ids_ref
  22.1 0.0 copy-done.3
  22.1 0.7 compare_convert_fusion.valid_ref
  22.8 0.0 copy-start.6
  22.8 331.6 %shard_map.100 = bf16[1024,1280]{1,0:T(8,128)(2,1)} custom-call(bf16[640,3840]{1,0:T(8,128)(2,1)} %pad_maximum_fusion.part_ref, bf16[1280,640]{1,0:T(8,128)(2,1)} %w_ref.1, s32[8,128,1]{2,1,0:T(8,128)} %copy.11.ids_ref, f32[8,128,1]{2,1,0:T(8,128)} %copy.12.inv_ref, s32[8,1,128]{2,1,0:T(1,128)} %compare_convert_fusion.valid_ref), custom_call_target="tpu_custom_call" | custom-call | flops 13421772800 | bytes 52428800 | tf_op jit(solution)/shard_map/pallas_call | solution.py:477
  354.3 0.0 copy-done.6
  354.4 0.6 dynamic_slice.15
  354.9 0.6 iota_compare_fusion.3
  355.6 0.1 fusion.3
  355.7 4.8 %select_convert_fusion = bf16[1024,1280]{1,0:T(8,128)(2,1)} fusion(bf16[1024,1280]{1,0:T(8,128)(2,1)} %shard_map.100, bf16[1024,5120]{1,0:T(8,128)(2,1)} %get-tuple-element.6, s32[]{:T(128)S(6)} %select_n.16, pred[1024]{0:T(1024)(128)(4,1)S(1)} %fusion.3), kind=kLoop, calls=%fused_computation.3 | loop fusion | flops 6553600 | bytes 7865348 | tf_op jit(solution)/shard_map/convert_element_type | solution.py:556
  (2 shorter events, 0.0 us)
Async XLA Ops:
  0.0 3.0 copy-start
  3.0 1.5 copy-start.4
  4.5 1.5 copy-start.5
  5.9 4.4 %slice-start = ((s8[5242880]{0:T(1024)(128)(4,1)}), s8[4194304]{0:T(1024)(128)(4,1)S(1)}, s32[]{:S(2)}) async-start(s8[5242880]{0:T(1024)(128)(4,1)} %bitcast.16), calls=%async_computation | async-start | bytes 8388608
  7.4 2.7 copy-start.1
  7.4 2.9 slice-start.1
  10.1 0.7 copy-start.2
  10.8 11.3 %copy-start.3 = (s32[8]{0:T(128)S(1)}, s32[8]{0:T(128)}, u32[]{:S(2)}) copy-start(s32[8]{0:T(128)} %param.11) | copy-start | bytes 100
  22.8 331.6 %copy-start.6 = (s32[8]{0:T(128)S(1)}, s32[8]{0:T(128)}, u32[]{:S(2)}) copy-start(s32[8]{0:T(128)} %param.12) | copy-start | bytes 100

commit v5 on v4

--- a/solution.py
+++ b/solution.py
@@ -108,7 +108,7 @@
 
     def order(self, c):
         levels = self.levels
-        return levels if c % 2 == 0 else (levels[1], levels[0]) + levels[2:]
+        return levels if c % 2 == 0 or c > 4 else (levels[1], levels[0]) + levels[2:]
 
     def span(self, c, level):
         low, size = 0, self.rows
@@ -124,7 +124,9 @@
             low, size = self.span(c, level)
             half = size // 2
             theirs = low + (1 - bit_of(self.me, bit)) * half
-            held = self.part if level == 0 else self.acc
+            if level:
+                theirs = theirs - self.span(c, 1)[0]
+            held = self.acc if level else self.part
             src = held.at[pl.ds(pl.multiple_of(theirs, 16), half), at]
             dst = self.land.at[pl.ds(self.rows - size, half), at]
         else:
@@ -147,21 +149,23 @@
             at = pl.ds(c * self.chunk, self.chunk)
             low, size = self.span(c, stage + 1)
             here = pl.ds(pl.multiple_of(low, 16), size)
-            mine = (self.part if stage == 0 else self.acc)[here, at].astype(jnp.float32)
+            kept = pl.ds(pl.multiple_of(low - self.span(c, 1)[0], 16), size)
+            mine = self.acc[kept, at] if stage else self.part[here, at]
+            mine = mine.astype(jnp.float32)
             got = self.land[pl.ds(self.rows - 2 * size, size), at].astype(jnp.float32)
             total = (mine + got).astype(jnp.bfloat16)
             if stage == self.count - 1:
                 self.out[here, at] = total
             else:
-                self.acc[here, at] = total
+                self.acc[kept, at] = total
 
     def run(self, beside=None):
         stages, ahead = 2 * self.count, 4
         for c in range(min(ahead, self.chunks)):
             self.start(c, 0)
         for step in range(stages + (self.chunks - 1) // 2):
-            if beside is not None and step == self.count:
-                beside()
+            if beside is not None:
+                beside(step)
             for c in range(self.chunks):
                 stage = step - c // 2
                 if 0 <= stage < stages:
@@ -205,7 +209,7 @@
         out_specs=whole,
         scratch_shapes=[
             pltpu.VMEM((rows, cols), jnp.bfloat16),
-            pltpu.VMEM((rows, cols), jnp.bfloat16),
+            pltpu.VMEM((rows // 2, cols), jnp.bfloat16),
             pltpu.SemaphoreType.DMA((chunks, 2 * count)),
             pltpu.SemaphoreType.DMA((chunks, 2 * count)),
         ],
@@ -232,7 +236,7 @@
         return self.weight[:, pl.ds(at, self.width)]
 
     def store(self, c, here, value):
-        self.out[here, pl.ds(c * self.width, self.width)] = value
+        self.out[here, pl.ds(c * self.width, self.width)] = value.astype(jnp.bfloat16)
 
     def product(self, c, mine, finish):
         tile = min(256, self.rows)
@@ -300,11 +304,11 @@
                 def _(t):
                     here = pl.ds(pl.multiple_of(t * tile, tile), tile)
                     got = self.land[c, 2 * self.half - 2 * size + k, here, :].astype(jnp.float32)
-                    value = (self.buf[c, low + k, here, :].astype(jnp.float32) + got).astype(jnp.bfloat16)
+                    value = self.buf[c, low + k, here, :].astype(jnp.float32) + got
                     if last:
                         self.store(c, here, value)
                     else:
-                        self.buf[c, low + k, here, :] = value
+                        self.buf[c, low + k, here, :] = value.astype(jnp.bfloat16)
 
     def advance(self, step):
         if step < self.chunks:
@@ -370,7 +374,7 @@
 
     def order(self, c):
         order = tuple(reversed(self.levels))
-        return order if c % 2 == 0 else order[:-2] + (order[-1], order[-2])
+        return order if c != 1 else order[:-2] + (order[-1], order[-2])
 
     def start(self, c, level):
         order = self.order(c)
@@ -403,12 +407,15 @@
         piece = self.weight.shape[-1]
         for q in range(self.width // piece):
             at = q * self.chunks * piece + c * piece
-            self.out[here, pl.ds(at, piece)] = value[:, q * piece:(q + 1) * piece]
+            full = self.out[here, pl.ds(at, piece)].astype(jnp.float32)
+            full = full + value[:, q * piece:(q + 1) * piece]
+            full = jnp.where(self.keep[here, :] != 0, full, 0.0)
+            self.out[here, pl.ds(at, piece)] = full.astype(jnp.bfloat16)
 
 
 def whole_kernel(
-    levels, count, heads, vocab, chunk, part_ref, w_ref, ids_ref, inv_ref, valid_ref, out_ref,
-    table, land, acc, held, mixed, buf, land_out, row_sems, held_sems, out_sems,
+    levels, count, heads, vocab, chunk, part_ref, w_ref, ids_ref, valid_ref, keep_ref,
+    embed_ref, position_ref, out_ref, table, land, acc, inv, held, mixed, buf, land_out, row_sems, held_sems, out_sems,
 ):
     me, part = lax.axis_index("row"), lax.axis_index("mp")
     sets, seq, _ = ids_ref.shape
@@ -419,17 +426,40 @@
     gather = Gather(me, levels, held, held_sems.at[0], held_sems.at[1])
     total = RowSum(me, levels, chunk, part_ref, table, land, acc, row_sems.at[0], row_sems.at[1])
     scatter = BlockScatter(part, count, mixed, held, out_ref, buf, land_out, out_sems.at[0], out_sems.at[1])
+    scatter.keep = keep_ref
     last = len(levels) - 1
-
-    def first():
+    d, features = embed_ref.shape[1], out_ref.shape[1]
+
+    def prepare(s):
+        columns = lax.broadcasted_iota(jnp.int32, (seq, vocab), 1)
+        pick = jnp.where(columns == ids_ref[s], 1.0, 0.0).astype(jnp.bfloat16)
+
+        def stored(at):
+            got = jnp.dot(pick, embed_ref[:, at], preferred_element_type=jnp.float32)
+            return (got + position_ref[:, at].astype(jnp.float32)).astype(jnp.bfloat16)
+
+        squares = jnp.zeros((seq, 1), jnp.float32)
+        for k in range(0, d, 512):
+            wide = stored(slice(k, min(k + 512, d))).astype(jnp.float32)
+            squares = squares + jnp.sum(wide * wide, axis=1, keepdims=True)
+        inv[s] = lax.rsqrt(squares / d + 1e-05)
+        here = pl.ds(pl.multiple_of(s * seq, seq), seq)
+        for k in range(0, features, 128):
+            at = pl.ds(pl.multiple_of(part * features + k, 128), 128)
+            out_ref[here, k:k + 128] = stored(at)
+
+    def beside(step):
+        if step == 0:
+            for c in range(chunks):
+                gather.start(c, 0)
+            pl.loop(0, sets)(prepare)
         for c in range(chunks):
-            gather.start(c, 0)
-
-    total.run(first)
-    for level in range(last - 1):
-        for c in range(chunks):
-            gather.finish(c, level)
-            gather.start(c, level + 1)
+            if step == (len(levels) + 1 if c < 2 else 2 * len(levels)):
+                for level in range(last - 1):
+                    gather.finish(c, level)
+                    gather.start(c, level + 1)
+
+    total.run(beside)
     pairs = [tuple(range(c, min(c + 2, chunks))) for c in range(0, chunks, 2)]
 
     def move(pair, level):
@@ -447,7 +477,7 @@
         def store(h, value):
             mixed[here, h * DH:(h + 1) * DH] = value
 
-        attend_set(heads, vocab, ids_ref[s], inv_ref[s], masked, table, store)
+        attend_set(heads, vocab, ids_ref[s], inv[s], masked, table, store)
 
     for n, pair in enumerate(pairs):
         if n + 1 < len(pairs):
@@ -459,9 +489,10 @@
         scatter.advance(step)
 
 
-def run_whole(partial, w_out, ids, inv, valid, row_count, part_count, heads, vocab):
+def run_whole(partial, w_out, ids, valid, keep, embed, position, row_count, part_count, heads):
     rows, cols = partial.shape
     sets, seq = ids.shape
+    vocab = embed.shape[0]
     depth, own = w_out.shape
     piece = 128
     chunks = own // piece
@@ -477,12 +508,13 @@
     return pl.pallas_call(
         functools.partial(whole_kernel, levels, count, heads, vocab, chunk),
         out_shape=jax.ShapeDtypeStruct((flat, features), jnp.bfloat16),
-        in_specs=[vmem] * 5,
+        in_specs=[vmem] * 7,
         out_specs=vmem,
         scratch_shapes=[
             pltpu.VMEM((rows, cols), jnp.bfloat16),
             pltpu.VMEM((rows, cols), jnp.bfloat16),
-            pltpu.VMEM((rows, cols), jnp.bfloat16),
+            pltpu.VMEM((rows // 2, cols), jnp.bfloat16),
+            pltpu.VMEM((sets, seq, 1), jnp.float32),
             pltpu.VMEM((chunks, row_count, depth, piece), jnp.bfloat16),
             pltpu.VMEM((flat, heads * DH), jnp.bfloat16),
             pltpu.VMEM((chunks, half, flat, width), jnp.bfloat16),
@@ -498,7 +530,7 @@
             flops=2 * flat * depth * own * row_count, bytes_accessed=2 * flat * depth * 20,
             transcendentals=0,
         ),
-    )(partial, w_out, ids[..., None], inv[..., None], valid[:, None, :])
+    )(partial, w_out, ids[..., None], valid[:, None, :], keep, embed, position)
 
 
 def on_device(
@@ -524,6 +556,19 @@
         for w in (w_query, w_key, w_value)
     ], axis=1)
 
+    live = jnp.arange(sets) < live_counts[me]
+    valid = jnp.arange(seq)[None, :] < set_lengths[:, None]
+    keep = (live[:, None] & valid).reshape(-1, 1)
+    aligned = (
+        w_out.shape[1] % 128 == 0 and partial.shape[1] % 640 == 0 and row_count == 8
+        and part_count >= 4
+    )
+    if aligned:
+        return run_whole(
+            partial, w_out, token_ids, valid.astype(jnp.int32), keep.astype(jnp.int32),
+            embed_table, position_table, row_count, part_count, heads,
+        ).reshape(sets, seq, -1)
+
     pick = (token_ids.reshape(-1, 1) == jnp.arange(vocab)[None]).astype(jnp.bfloat16)
     picked = jnp.dot(pick, embed_table, preferred_element_type=jnp.float32)
     stored = (
@@ -531,28 +576,14 @@
     ).astype(jnp.bfloat16)
     widened = stored.astype(jnp.float32)
     inv = lax.rsqrt(jnp.mean(widened * widened, axis=-1) + 1e-05)
-
-    live = jnp.arange(sets) < live_counts[me]
-    valid = jnp.arange(seq)[None, :] < set_lengths[:, None]
-    aligned = w_out.shape[1] % 128 == 0 and partial.shape[1] % 640 == 0
-    if aligned:
-        summed = run_whole(
-            partial, w_out, token_ids, inv, valid.astype(jnp.int32), row_count, part_count,
-            heads, vocab,
-        )
-    else:
-        table = sum_over_rows(partial, row_count)
-        out_full = lax.all_gather(w_out, "row", axis=1, tiled=True)
-        mixed = attend(
-            token_ids, set_lengths, live.astype(jnp.int32), inv, table, heads, vocab
-        )
-        summed = project_out(mixed, out_full, part_count)
-    summed = summed.astype(jnp.float32)
+    table = sum_over_rows(partial, row_count)
+    out_full = lax.all_gather(w_out, "row", axis=1, tiled=True)
+    mixed = attend(token_ids, set_lengths, live.astype(jnp.int32), inv, table, heads, vocab)
+    summed = project_out(mixed, out_full, part_count).astype(jnp.float32)
     features = summed.shape[1]
     residual = lax.dynamic_slice_in_dim(
         stored.reshape(sets * seq, d), part * features, features, 1
     ).astype(jnp.float32)
-    keep = (live[:, None] & valid).reshape(-1, 1)
     output = jnp.where(keep, residual + summed, 0.0).astype(jnp.bfloat16)
     return output.reshape(sets, seq, features)
 

time: 361 us -> 343 us (0.950)
  matrix products: 13.6 us -> 4.35 us
  Pallas kernels: 332 us -> 325 us
  other arithmetic: 9.12 us -> 3.94 us
    dot_general x1 -> x0, matrix products: 9.24 us -> none  [on_device(): picked = jnp.dot(pick, embed_table, preferred_element_type=jnp.float32)]
    pallas_call x1, Pallas kernels: 332 us -> 325 us  [run_whole(): pl.pallas_call(functools.partial(whole_kernel, levels, count, heads, voca...]
    convert_element_type x2 -> x1, other arithmetic: 5.07 us -> 0.07 us  [on_device(): keep.astype(jnp.int32)]
where the time goes in v5:
time: 343 us
  Pallas kernels  325 us (95%)
  local copies, waits for them, and re-layouts  9.07 us (3%)
  matrix products  4.35 us (1%)
  other arithmetic  3.94 us (1%)
    pallas_call x1, Pallas kernels, run_whole(): pl.pallas_call(functools.partial(whole_kernel, levels, count, heads, voca...  325 us

profile of v5, /device:TPU:0, one launch (start us, length us, event | category | flops | bytes accessed | tf_op | source)
XLA Modules:
  0.0 342.7 jit_solution(8751345333696447231)
XLA Ops:
  0.0 0.0 copy-start
  0.0 1.3 constant_dynamic-slice_fusion.1
  1.3 0.9 constant_dynamic-slice_fusion
  2.2 0.8 dynamic_slice.14
  3.0 0.0 copy-done
  3.0 0.0 copy-start.3
  3.0 1.4 convolution_convert_fusion.1
  4.5 0.0 copy-done.3
  4.5 0.0 copy-start.4
  4.5 1.5 convolution_convert_fusion.2
  5.9 0.0 copy-done.4
  5.9 1.5 convolution_convert_fusion
  7.4 0.0 copy-start.5
  7.4 0.0 copy-start.2
  7.4 0.0 copy-start.1
  7.4 2.6 pad_maximum_fusion.part_ref
  10.0 0.0 copy-done.5
  10.0 0.6 dynamic_slice.15
  10.6 0.6 iota_compare_fusion.1
  11.2 0.0 copy-done.2
  11.2 0.1 fusion.1
  11.3 1.0 copy.12.keep_ref
  12.3 0.0 copy-done.1
  12.3 1.0 copy.11.ids_ref
  13.4 0.7 compare_convert_fusion.valid_ref
  14.0 325.2 %shard_map.100 = bf16[1024,1280]{1,0:T(8,128)(2,1)} custom-call(bf16[640,3840]{1,0:T(8,128)(2,1)} %pad_maximum_fusion.part_ref, bf16[1280,640]{1,0:T(8,128)(2,1)} %w_ref.1, s32[8,128,1]{2,1,0:T(8,128)} %copy.11.ids_ref, s32[8,1,128]{2,1,0:T(1,128)} %compare_convert_fusion.valid_ref, s32[1024,1]{1,0:T(8,128)} %copy.12.keep_ref, bf16[512,5120]{1,0:T(8,128)(2,1)} %embed_ref.1, ...), custom_call_target="tpu_custom_call" | custom-call | flops 13421772800 | bytes 52428800 | tf_op jit(solution)/shard_map/pallas_call | solution.py:508
  339.2 3.4 copy.14
Async XLA Ops:
  0.0 3.0 copy-start
  3.0 1.5 copy-start.3
  4.5 1.5 copy-start.4
  7.4 2.6 copy-start.5
  7.4 3.8 %copy-start.2 = (s32[8]{0:T(128)S(1)}, s32[8]{0:T(128)}, u32[]{:S(2)}) copy-start(s32[8]{0:T(128)} %param.11) | copy-start | bytes 100
  7.4 4.9 %copy-start.1 = (s32[8,128]{1,0:T(8,128)S(1)}, s32[8,128]{1,0:T(8,128)}, u32[]{:S(2)}) copy-start(s32[8,128]{1,0:T(8,128)} %param.10) | copy-start | bytes 12292
